TPU v7x, 32 devices: a whole 2x2x4 slice. The times are simulated.
32 devices in a mesh: row: 4 (over y, core), col: 4 (over z), seq: 2 (over x).
Axes of the slice: x: 2, y: 2, z: 4, core: 2. Of those that a mesh axis runs over, the one named last changes fastest.
Arguments:
- queries: bfloat16 [4, 2048, 8192], P('row', 'seq', 'col'), may hold values from -120 to 120
- rotated_key_heads: bfloat16 [4, 2048, 1024], P('row', 'seq', 'col'), may hold values from -7 to 7
- value_head_states: bfloat16 [4, 2048, 1024], P('row', 'seq', 'col'), may hold values from -6 to 6
- document_index: int32 [4, 2048], P('row'), may hold values from 0 to 3, never falling along the last dimension, each value on 1 to 1024 neighbouring positions
- output_projection_weight: bfloat16 [8192, 8192], P('col', 'row'), may hold values from -0.1875 to 0.1875
- frozen_down_factor: bfloat16 [8192, 256], P('col'), may hold values from -0.1875 to 0.1875
- trained_up_factor: bfloat16 [256, 8192], P(None, 'row'), may hold values from -0.125 to 0.125
- correction_tiles: bfloat16 [4, 4, 5, 128, 128], P('row', 'col'), may hold values from -1.1953125 to 1.1953125
- tile_placement: int32 [4, 4, 5, 2], P('row', 'col'), may hold values from 0 to 15, as said below
- cotangent: bfloat16 [4, 2048, 8192], P(None, 'seq', ('row', 'col')), may hold values from -0.06591797 to 0.06591797
Outputs:
- projected: bfloat16 [4, 2048, 8192], P(None, 'seq', ('row', 'col'))
- up_factor_gradient: float32 [256, 8192], P(None, 'row')
- grad_tiles: float32 [4, 4, 5, 128, 128], P('row', 'col')
Inputs may be any that keep to these rules, and one draw needn't show every extreme that they name: `tile_placement`: inside one block of the weight grid the 5 tiles are different; entry 0 is a tile row below 16, entry 1 a tile column below 16.
All inputs are finite; a program needn't handle non-finite values.
Results may differ from a plain program's by a relative error of at most 0.0054.
Values may be sent and summed in bfloat16 or wider, within the bound.
No kernel may reach another device: no remote copies, remote signals or barrier semaphores. Data moves between devices by JAX's collectives and lax.ppermute only.
A program may use at most 192 MiB of HBM per device.

v0:
```python
import jax
import jax.numpy as jnp
from jax import lax
from jax.sharding import PartitionSpec as P

QUERY_HEADS = 64
KEY_VALUE_HEADS = 8
HEAD_WIDTH = 128
TILE = 128


low_rank_factor = 2.0


def attend(queries, key_rows, values, documents, query_start):
    item_count, query_len, shared_heads, query_group_width, head_size = queries.shape
    key_len = key_rows.shape[1]
    block_rows = min(512, query_len)
    block_count = query_len // block_rows
    score_scale = head_size ** (-0.5)
    key_pos = jnp.arange(key_len, dtype=jnp.int32)

    def one_block(block_index):
        row_start = block_index * block_rows
        query_part = lax.dynamic_slice_in_dim(queries, row_start, block_rows, 1)
        scores = (
            jnp.einsum(
                "nqkgd,nskd->nkgqs", query_part, key_rows, preferred_element_type=jnp.float32
            )
            * score_scale
        )
        query_pos = query_start + row_start + jnp.arange(block_rows, dtype=jnp.int32)
        query_docs = lax.dynamic_slice_in_dim(documents, query_start + row_start, block_rows, 1)
        visible = (key_pos[None, None, :] <= query_pos[None, :, None]) & (
            documents[:, None, :] == query_docs[:, :, None]
        )
        visible = visible[:, None, None, :, :]
        row_max = jnp.max(jnp.where(visible, scores, -jnp.inf), axis=-1, keepdims=True)
        weights = jnp.exp(jnp.where(visible, scores - row_max, -jnp.inf))
        row_total = jnp.sum(weights, axis=-1)
        mixed_rows = jnp.einsum(
            "nkgqs,nskd->nqkgd",
            weights.astype(jnp.bfloat16),
            values,
            preferred_element_type=jnp.float32,
        )
        mixed_rows = mixed_rows / jnp.moveaxis(row_total, 3, 1)[..., None]
        return mixed_rows.astype(jnp.bfloat16)

    results = lax.map(one_block, jnp.arange(block_count, dtype=jnp.int32))
    return jnp.moveaxis(results, 0, 1).reshape(
        item_count, query_len, shared_heads * query_group_width * head_size
    )


def local(
    queries,
    rotated_key_heads,
    value_head_states,
    document_index,
    output_projection_weight,
    frozen_down_factor,
    trained_up_factor,
    correction_tiles,
    tile_placement,
    cotangent,
):
    leading = queries.shape[0]
    local_len = queries.shape[1]
    col_width = queries.shape[2]
    shared_col = rotated_key_heads.shape[2] // HEAD_WIDTH
    query_group_width = QUERY_HEADS // KEY_VALUE_HEADS
    key_full, value_full = (
        lax.all_gather(rotated_key_heads, "seq", axis=1, tiled=True),
        lax.all_gather(value_head_states, "seq", axis=1, tiled=True),
    )
    full_len = key_full.shape[1]
    shaped = queries.reshape(leading, local_len, shared_col, query_group_width, HEAD_WIDTH)
    attention_output = attend(
        shaped,
        key_full.reshape(leading, full_len, shared_col, HEAD_WIDTH),
        value_full.reshape(leading, full_len, shared_col, HEAD_WIDTH),
        document_index,
        lax.axis_index("seq") * local_len,
    )
    gathered = lax.all_gather(attention_output, "row", axis=0, tiled=True)
    sequence_rows = gathered.shape[0]
    seq_total = sequence_rows * local_len
    flattened_rows = gathered.reshape(seq_total, col_width)
    out_width = output_projection_weight.shape[1]
    in_tiles = col_width // TILE
    out_tiles = out_width // TILE
    coords = tile_placement.reshape(-1, 2)
    tile_in = coords[:, 0]
    tile_out = coords[:, 1]
    tile_values = correction_tiles.reshape(-1, TILE, TILE)
    partial_value = jnp.dot(
        flattened_rows, output_projection_weight, preferred_element_type=jnp.float32
    )
    low_rank_piece = jnp.dot(flattened_rows, frozen_down_factor, preferred_element_type=jnp.float32)
    picked = flattened_rows.reshape(seq_total, in_tiles, TILE)[:, tile_in]
    tile_terms = jnp.einsum("tbi,bio->tbo", picked, tile_values, preferred_element_type=jnp.float32)
    partial_value = (
        partial_value.reshape(seq_total, out_tiles, TILE)
        .at[:, tile_out]
        .add(tile_terms)
        .reshape(seq_total, out_width)
    )
    combined_output = lax.psum_scatter(
        partial_value.reshape(sequence_rows, local_len, out_width),
        "col",
        scatter_dimension=2,
        tiled=True,
    )
    low_rank_inner = lax.psum(low_rank_piece, "col").astype(jnp.bfloat16)
    segment_width = combined_output.shape[2]
    up_factor_piece = lax.dynamic_slice_in_dim(
        trained_up_factor, lax.axis_index("col") * segment_width, segment_width, 1
    )
    combined_output = combined_output + low_rank_factor * jnp.dot(
        low_rank_inner, up_factor_piece, preferred_element_type=jnp.float32
    ).reshape(combined_output.shape)
    cot_full = lax.all_gather(cotangent, "col", axis=2, tiled=True)
    cot_flat = cot_full.reshape(seq_total, out_width)
    cot_picked = cot_flat.reshape(seq_total, out_tiles, TILE)[:, tile_out]
    tile_grad = jnp.einsum("tbi,tbo->bio", picked, cot_picked, preferred_element_type=jnp.float32)
    up_factor_block = low_rank_factor * lax.dot_general(
        low_rank_inner, cot_flat, (((0,), (0,)), ((), ())), preferred_element_type=jnp.float32
    )
    up_factor_gradient, tile_total = lax.psum((up_factor_block, tile_grad), "seq")
    return (
        combined_output.astype(jnp.bfloat16),
        up_factor_gradient,
        tile_total.reshape(correction_tiles.shape),
    )


def solution(mesh):
    placed = (
        P("row", "seq", "col"),
        P("row", "seq", "col"),
        P("row", "seq", "col"),
        P("row", None),
        P("col", "row"),
        P("col", None),
        P(None, "row"),
        P("row", "col", None, None, None),
        P("row", "col", None, None),
        P(None, "seq", ("row", "col")),
    )
    return jax.shard_map(
        local,
        mesh=mesh,
        in_specs=placed,
        out_specs=(
            P(None, "seq", ("row", "col")),
            P(None, "row"),
            P("row", "col", None, None, None),
        ),
        check_vma=False,
    )
```

profile of v0, /device:TPU:0, one launch (start us, length us, event | category | flops | bytes accessed | tf_op | source)
XLA Modules:
  0.0 1386.3 jit_solution(16464379851530381612)
XLA Ops:
  11.6 6.4 copy.28
  18.0 16.2 %all-gather.5.cloned.1.call-done = bf16[1,2048,256]{1,2,0:T(8,128)(2,1)} async-done(((bf16[1,1024,256]{1,2,0:T(8,128)(2,1)}), bf16[1,2048,256]{1,2,0:T(8,128)(2,1)}) %all-gather.5.cloned.1.call-update) | async-done | bytes 1048592 | tf_op jit(solution)/shard_map/all_gather | solution.py:74
  35.8 21.3 %all-gather.7.cloned.1.call-done = bf16[1,2048,256]{1,2,0:T(8,128)(2,1)} async-done(((bf16[1,1024,256]{1,2,0:T(8,128)(2,1)}), bf16[1,2048,256]{1,2,0:T(8,128)(2,1)}) %all-gather.7.cloned.1.call-update) | async-done | bytes 1048592 | tf_op jit(solution)/shard_map/all_gather | solution.py:75
  58.7 153.6 %while.11 = (s32[]{:T(128)}, bf16[2,1,512,2,8,128]{5,4,3,2,0,1:T(8,128)(2,1)}, s32[2]{0:T(128)S(1)}, s32[]{:T(128)}, s32[1,2048]{1,0:T(1,128)S(1)}, /*index=5*/b...) while((s32[]{:T(128)}, ...), condition=%wide.region_3.4_spmd.clone, body=%wide.region_0.3_spmd.clone.sunk | while | flops 8779710464 | bytes 216189168 | solution.py:50
  61.0 26.3 %fusion.61 = (f32[2,8,512]{2,1,0:T(8,128)S(1)}, f32[2,512,8,2048]{3,1,2,0:T(8,128)}) fusion(pred[512,2048]{1,0:T(8,128)(4,1)S(1)} %fusion.60, bf16[1,2048,2,128]{3,1,2,0:T(8,128)(2,1)S(1)} %get-tuple-element.194, bf16[1,1024,2,8,128]{1,4,3,2,0:T(8,128)(2,1)} %get-tuple-element.193, s32[]{:T(128)S(6)} %select_n.64), kind=kOutput, calls=%fused_computation.6.clone.1 | convolution fusion | flops 4345290752 | bytes 71335936 | tf_op jit(solution)/shard_map/while/body/eval_jaxpr/nqkgd,nskd->nkgqs/dot_general | solution.py:27
  87.4 21.5 %fusion.62 = f32[2,8,512]{2,1,0:T(8,128)S(1)} fusion(f32[2,512,8,2048]{3,1,2,0:T(8,128)} %get-tuple-element.160, f32[2,8,512]{2,1,0:T(8,128)S(1)} %get-tuple-element.161, pred[512,2048]{1,0:T(8,128)(4,1)S(1)} %fusion.60), kind=kLoop, calls=%fused_computation.9.clone.1 | loop fusion | flops 67100672 | bytes 68222976 | tf_op jit(solution)/shard_map/while/body/eval_jaxpr/reduce_sum | solution.py:40
  108.9 23.9 %fusion.63 = bf16[1,1,512,2,8,128]{5,2,4,3,1,0:T(8,128)(2,1)S(1)} fusion(f32[512,2,8]{0,2,1:T(8,128)S(1)} %bitcast.161, f32[2,512,8,2048]{3,1,2,0:T(8,128)} %get-tuple-element.160, f32[2,8,512]{2,1,0:T(8,128)S(1)} %get-tuple-element.161, pred[512,2048]{1,0:T(8,128)(4,1)S(1)} %fusion.60, bf16[1,2048,2,128]{3,1,2,0:T(8,128)(2,1)S(1)} %get-tuple-element.195), kind=kOutput, calls=%fused_computation.22.clone.1 | convolution fusion | flops 4364173312 | bytes 71368704 | tf_op jit(solution)/shard_map/while/body/eval_jaxpr/nkgqs,nskd->nqkgd/dot_general | solution.py:41
  137.8 26.3 %fusion.61 = (f32[2,8,512]{2,1,0:T(8,128)S(1)}, f32[2,512,8,2048]{3,1,2,0:T(8,128)}) fusion(pred[512,2048]{1,0:T(8,128)(4,1)S(1)} %fusion.60, bf16[1,2048,2,128]{3,1,2,0:T(8,128)(2,1)S(1)} %get-tuple-element.194, bf16[1,1024,2,8,128]{1,4,3,2,0:T(8,128)(2,1)} %get-tuple-element.193, s32[]{:T(128)S(6)} %select_n.64), kind=kOutput, calls=%fused_computation.6.clone.1 | convolution fusion | flops 4345290752 | bytes 71335936 | tf_op jit(solution)/shard_map/while/body/eval_jaxpr/nqkgd,nskd->nkgqs/dot_general | solution.py:27
  164.2 21.5 %fusion.62 = f32[2,8,512]{2,1,0:T(8,128)S(1)} fusion(f32[2,512,8,2048]{3,1,2,0:T(8,128)} %get-tuple-element.160, f32[2,8,512]{2,1,0:T(8,128)S(1)} %get-tuple-element.161, pred[512,2048]{1,0:T(8,128)(4,1)S(1)} %fusion.60), kind=kLoop, calls=%fused_computation.9.clone.1 | loop fusion | flops 67100672 | bytes 68222976 | tf_op jit(solution)/shard_map/while/body/eval_jaxpr/reduce_sum | solution.py:40
  185.7 23.9 %fusion.63 = bf16[1,1,512,2,8,128]{5,2,4,3,1,0:T(8,128)(2,1)S(1)} fusion(f32[512,2,8]{0,2,1:T(8,128)S(1)} %bitcast.161, f32[2,512,8,2048]{3,1,2,0:T(8,128)} %get-tuple-element.160, f32[2,8,512]{2,1,0:T(8,128)S(1)} %get-tuple-element.161, pred[512,2048]{1,0:T(8,128)(4,1)S(1)} %fusion.60, bf16[1,2048,2,128]{3,1,2,0:T(8,128)(2,1)S(1)} %get-tuple-element.195), kind=kOutput, calls=%fused_computation.22.clone.1 | convolution fusion | flops 4364173312 | bytes 71368704 | tf_op jit(solution)/shard_map/while/body/eval_jaxpr/nkgqs,nskd->nqkgd/dot_general | solution.py:41
  212.3 7.3 reshape_transpose.3
  220.3 12.8 copy.45
  233.7 92.1 %all-gather.9.cloned.1.call-done = bf16[4,1024,2048]{2,1,0:T(8,128)(2,1)} async-done(((bf16[1,1024,2048]{2,1,0:T(8,128)(2,1)}), bf16[4,1024,2048]{2,1,0:T(8,128)(2,1)}) %all-gather.9.cloned.1.call-update) | async-done | bytes 16777232 | tf_op jit(solution)/shard_map/all_gather | solution.py:86
  325.7 15.8 %copy.51 = bf16[512,8,16,128]{3,2,1,0:T(8,128)(2,1)} copy(bf16[512,8,16,128]{3,1,2,0:T(8,128)(2,1)} %bitcast.153) | data formatting | bytes 33554432
  341.5 22.4 %copy.46 = bf16[4096,16,128]{0,2,1:T(8,128)(2,1)} copy(bf16[4096,16,128]{2,1,0:T(8,128)(2,1)} %bitcast.150) | data formatting | bytes 33554432 | tf_op jit(solution)/shard_map/reshape;reshape | solution.py:101
  363.9 9.7 gather_fusion
  373.6 8.4 fusion.28
  382.0 41.0 %fusion.43 = f32[4096,16,128]{2,0,1:T(8,128)} fusion(bf16[4096,2048,1]{1,0,2:T(8,128)(2,1)} %bitcast.154, bf16[16,128,2048]{2,1,0:T(8,128)(2,1)S(1)} %bitcast.157), kind=kOutput, calls=%fused_computation.50 | convolution fusion | flops 34359738368 | bytes 58720256 | tf_op jit(solution)/shard_map/dot_general | solution.py:97
  423.0 19.5 %scatter_fusion = f32[4096,16,128]{2,0,1:T(8,128)} fusion(f32[4096,16,128]{2,0,1:T(8,128)} %fusion.43, s32[5]{0:T(128)S(1)} %get-tuple-element.106, f32[5,4096,128]{2,1,0:T(8,128)} %fusion.28), kind=kCustom, calls=%fused_computation.2 | custom fusion | flops 2621440 | bytes 31457300 | tf_op jit(solution)/shard_map/scatter-add | solution.py:106
  442.5 32.1 %copy.38 = f32[4096,16,128]{2,1,0:T(8,128)} copy(f32[4096,16,128]{2,0,1:T(8,128)} %scatter_fusion) | data formatting | bytes 67108864 | tf_op jit(solution)/shard_map/scatter-add | solution.py:106
  474.6 35.5 %reshape_reshape.10 = f32[4,1024,2048]{2,1,0:T(8,128)} reshape(f32[4096,16,128]{2,1,0:T(8,128)} %copy.38) | data formatting | bytes 67108864 | tf_op jit(solution)/shard_map/reshape;reshape | solution.py:110
  510.2 103.8 %all-gather.11.cloned.1.call-done = bf16[4,1024,2048]{2,1,0:T(8,128)(2,1)} async-done(((bf16[4,1024,512]{2,1,0:T(8,128)(2,1)}), bf16[4,1024,2048]{2,1,0:T(8,128)(2,1)}) %all-gather.11.cloned.1.call-update) | async-done | bytes 16777232 | tf_op jit(solution)/shard_map/all_gather | solution.py:123
  614.0 15.2 %copy.52 = bf16[512,8,16,128]{3,2,1,0:T(8,128)(2,1)} copy(bf16[512,8,16,128]{3,1,2,0:T(8,128)(2,1)} %bitcast.146) | data formatting | bytes 33554432
  629.1 22.2 %copy.47 = bf16[4096,16,128]{0,2,1:T(8,128)(2,1)} copy(bf16[4096,16,128]{2,1,0:T(8,128)(2,1)} %bitcast.151) | data formatting | bytes 33554432 | tf_op jit(solution)/shard_map/reshape;reshape | solution.py:125
  651.3 10.0 gather_fusion.1
  661.3 10.4 fusion.44
  673.9 280.7 %all-reduce.5 = bf16[4096,256]{1,0:T(8,128)(2,1)S(1)} all-reduce(f32[4096,256]{1,0:T(8,128)} %fusion.44), channel_id=1, replica_groups=mesh['row'=4,'col'=4,'seq'=2] {'col'}, use_global_device_ids=true, to_apply=%region_6.7 | all-reduce | flops 1048576 | bytes 6291456 | tf_op jit(solution)/shard_map/psum | solution.py:115
  954.6 9.9 convolution_multiply_fusion.1
  964.6 4.5 convolution_multiply_fusion
  969.1 331.2 %reduce-scatter.2.cloned.1.call-done = f32[4,1024,512]{2,1,0:T(8,128)} async-done(((f32[4,1024,2048]{2,1,0:T(8,128)}), f32[4,1024,512]{2,1,0:T(8,128)}) %reduce-scatter.2.cloned.1.call-update) | async-done | bytes 8388624 | tf_op jit(solution)/shard_map/reduce_scatter | solution.py:109
  1300.2 9.3 add_convert_fusion
  1309.5 64.7 %all-reduce.4.cloned.1.call-done = (f32[256,2048]{1,0:T(8,128)}, f32[1,1,5,128,128]{4,3,2,1,0:T(8,128)}) async-done(((f32[256,2048]{1,0:T(8,128)}, f32[1,1,5,128,128]{4,3,2,1,0:T(8,128)}), (f32[256,2048]{1,0:T(8,128)}, f32[1,1,5,128,128]{4,3,2,1,0:T(8,128)})) %all-reduce.4.cloned.1.call-update) | async-done | bytes 2424848 | tf_op jit(solution)/shard_map/psum | solution.py:130
  (52 shorter events, 24.6 us)
Async XLA Ops:
  7.2 957.4 %copy-start = (bf16[256,2048]{1,0:T(8,128)(2,1)S(1)}, bf16[256,2048]{1,0:T(8,128)(2,1)}, u32[]{:S(2)}) copy-start(bf16[256,2048]{1,0:T(8,128)(2,1)} %param.18) | copy-start | bytes 3145732
  7.2 51.5 %copy-start.3 = (s32[1,2048]{1,0:T(1,128)S(1)}, s32[1,2048]{1,0:T(1,128)}, u32[]{:S(2)}) copy-start(s32[1,2048]{1,0:T(1,128)} %param.15) | copy-start | bytes 24580
  7.2 27.0 %all-gather.5.cloned.1.call-start = ((), (), s32[]{:S(2)}) async-start(), calls=%async_computation.1 | async-start | bytes 1572864 | tf_op jit(solution)/shard_map/all_gather | solution.py:74
  9.4 47.7 %all-gather.7.cloned.1.call-start = ((), (), s32[]{:S(2)}) async-start(), calls=%async_computation.2 | async-start | bytes 1572864 | tf_op jit(solution)/shard_map/all_gather | solution.py:75
  11.5 314.2 %all-gather.9.cloned.1.call-start = ((), (), s32[]{:S(2)}) async-start(), calls=%async_computation.3 | async-start | bytes 20971520 | tf_op jit(solution)/shard_map/all_gather | solution.py:86
  219.7 394.3 %all-gather.11.cloned.1.call-start = ((), (), s32[]{:S(2)}) async-start(), calls=%async_computation.5 | async-start | bytes 20971520 | tf_op jit(solution)/shard_map/all_gather | solution.py:123
  220.2 1080.0 %reduce-scatter.2.cloned.1.call-start = ((), (), s32[]{:S(2)}) async-start(), calls=%async_computation.4 | async-start | bytes 41943040 | tf_op jit(solution)/shard_map/reduce_scatter | solution.py:109
  220.3 12.8 copy-start.5
  363.9 9.7 copy-start.4
  373.6 8.5 copy-start.2
  510.1 864.1 %all-reduce.4.cloned.1.call-start = ((), (), s32[]{:S(2)}) async-start(), calls=%async_computation.6 | async-start | bytes 4849664 | tf_op jit(solution)/shard_map/psum | solution.py:130
  651.3 10.0 copy-start.6
  651.3 20.3 %slice-start = ((s8[5242880]{0:T(1024)(128)(4,1)}), s8[1048576]{0:T(1024)(128)(4,1)S(1)}, s32[]{:S(2)}) async-start(s8[5242880]{0:T(1024)(128)(4,1)} %bitcast.148), calls=%async_computation.7 | async-start | bytes 2097152
  661.3 10.4 slice-start.1
  661.3 10.4 copy-start.1
Sparse Core Ops, SparseCore 0:
  10.1 23.9 all-gather.4
  35.7 21.2 all-gather.6
  219.8 105.9 all-gather.8
  327.2 286.7 all-gather.10
  616.2 684.0 reduce-scatter.1
  1303.2 70.9 all-reduce.3
where the time goes:
time: 1400 us; the launch traced here: 1390 us
  waiting for transfers between devices  630 us (45%)
  blocking collectives  281 us (20%)
  local copies, waits for them, and re-layouts  208 us (15%)
  matrix products  177 us (13%)
  other arithmetic  74.5 us (5%)
  between operations  14.7 us (1%)
    reduce_scatter x1, waiting for transfers between devices, local(): lax.psum_scatter(partial_value.reshape(sequence_rows, local_len, out_widt...  331 us
    psum x1, blocking collectives, local(): low_rank_inner = lax.psum(low_rank_piece, 'col').astype(jnp.bfloat16)  281 us
    all_gather x1, waiting for transfers between devices, local(): cot_full = lax.all_gather(cotangent, 'col', axis=2, tiled=True)  104 us
    all_gather x1, waiting for transfers between devices, local(): gathered = lax.all_gather(attention_output, 'row', axis=0, tiled=True)  92.1 us
    psum x1, waiting for transfers between devices, local(): lax.psum((up_factor_block, tile_grad), 'seq')  64.7 us
    dot_general x2, matrix products, one_block(): jnp.einsum('nqkgd,nskd->nkgqs', query_part, key_rows, preferred_element_t...  52.7 us
    unnamed x27, local copies, waits for them, and re-layouts  49.7 us
    dot_general x2, matrix products, one_block(): jnp.einsum('nkgqs,nskd->nqkgd', weights.astype(jnp.bfloat16), values, pre...  47.9 us
  transfers between devices with their start and end apart: 6, of which 6 were waited for; matrix products, arithmetic and copies ran while one was open for 21% of the time, Pallas kernels for 0%

commit v1 on v0

v1 whole, which is shorter than its diff:
```python
import functools

import jax
import jax.numpy as jnp
from jax import lax
from jax.experimental import pallas as pl
from jax.experimental.pallas import tpu as pltpu
from jax.sharding import PartitionSpec as P

HEAD_WIDTH = 128
TILE = 128
F32 = jnp.float32
BF16 = jnp.bfloat16
LOW_RANK_FACTOR = 2.0
NEG = -1e30
LOG2E = 1.4426950408889634


def attend_kernel(bounds_ref, q_ref, k_ref, vt_ref, start_ref, o_ref, *, heads, key_block, first, blocks):
    rows = q_ref.shape[0]
    block = first + pl.program_id(2)
    scale = HEAD_WIDTH ** (-0.5) * LOG2E
    starts = start_ref[...]
    positions = bounds_ref[2 * blocks] + block * rows + lax.broadcasted_iota(jnp.int32, (1, rows), 1)
    queries = [q_ref[:, h * HEAD_WIDTH:(h + 1) * HEAD_WIDTH] for h in range(heads)]

    def step(at, carry):
        base = pl.multiple_of(at * key_block, key_block)
        keys = k_ref[pl.ds(base, key_block), :]
        values = vt_ref[:, pl.ds(base, key_block)]
        key_pos = base + lax.broadcasted_iota(jnp.int32, (key_block, rows), 0)
        visible = (key_pos >= starts) & (key_pos <= positions)
        out = []
        for h in range(heads):
            top, total, acc = carry[h]
            scores = lax.dot_general(
                keys, queries[h], (((1,), (1,)), ((), ())), preferred_element_type=F32
            )
            scores = jnp.where(visible, scores * scale, NEG)
            new_top = jnp.maximum(top, jnp.max(scores, axis=0, keepdims=True))
            probs = jnp.exp2(scores - new_top)
            fade = jnp.exp2(top - new_top)
            total = total * fade + jnp.sum(probs, axis=0, keepdims=True)
            acc = acc * fade + jnp.dot(values, probs.astype(BF16), preferred_element_type=F32)
            out.append((new_top, total, acc))
        return tuple(out)

    start = tuple(
        (
            jnp.full((1, rows), NEG, F32),
            jnp.zeros((1, rows), F32),
            jnp.zeros((HEAD_WIDTH, rows), F32),
        )
        for _ in range(heads)
    )
    done = lax.fori_loop(bounds_ref[block], bounds_ref[blocks + block], step, start)
    for h in range(heads):
        _, total, acc = done[h]
        o_ref[:, h * HEAD_WIDTH:(h + 1) * HEAD_WIDTH] = jnp.transpose(acc / total).astype(BF16)


def attend_chunk(queries, keys, values_t, bounds, starts, offset, rows, block_rows, key_block):
    length, width = queries.shape
    key_len = keys.shape[0]
    kv_heads = keys.shape[1] // HEAD_WIDTH
    group = width // HEAD_WIDTH // kv_heads
    heads = min(4, group)
    steps = group // heads
    first = offset // block_rows
    grid_spec = pltpu.PrefetchScalarGridSpec(
        num_scalar_prefetch=1,
        grid=(kv_heads, steps, rows // block_rows),
        in_specs=[
            pl.BlockSpec((block_rows, heads * HEAD_WIDTH), lambda g, s, i, b: (first + i, g * steps + s)),
            pl.BlockSpec((key_len, HEAD_WIDTH), lambda g, s, i, b: (0, g)),
            pl.BlockSpec((HEAD_WIDTH, key_len), lambda g, s, i, b: (g, 0)),
            pl.BlockSpec((1, block_rows), lambda g, s, i, b: (0, first + i)),
        ],
        out_specs=pl.BlockSpec((block_rows, heads * HEAD_WIDTH), lambda g, s, i, b: (i, g * steps + s)),
    )
    work = rows * key_len // 3 * width
    return pl.pallas_call(
        functools.partial(
            attend_kernel, heads=heads, key_block=key_block, first=first, blocks=length // block_rows
        ),
        out_shape=jax.ShapeDtypeStruct((rows, width), BF16),
        grid_spec=grid_spec,
        compiler_params=pltpu.CompilerParams(vmem_limit_bytes=32 * 1024 * 1024),
        cost_estimate=pl.CostEstimate(
            flops=8 * work, bytes_accessed=4 * rows * width, transcendentals=work // HEAD_WIDTH
        ),
        name="attention",
    )(bounds, queries, keys, values_t, starts)


def add_tiles_kernel(in_ref, out_tile_ref, w_ref, tiles_ref, o_ref):
    o_ref[...] = w_ref[...]
    for t in range(tiles_ref.shape[0]):

        @pl.when(in_ref[t] == pl.program_id(0))
        def _(t=t):
            at = pl.ds(pl.multiple_of(out_tile_ref[t] * TILE, TILE), TILE)
            o_ref[:, at] = (o_ref[:, at].astype(F32) + tiles_ref[t].astype(F32)).astype(BF16)


def add_tiles(weight, tiles, tile_in, tile_out):
    depth, out_width = weight.shape
    grid_spec = pltpu.PrefetchScalarGridSpec(
        num_scalar_prefetch=2,
        grid=(depth // TILE,),
        in_specs=[
            pl.BlockSpec((TILE, out_width), lambda i, ti, to: (i, 0)),
            pl.BlockSpec(tiles.shape, lambda i, ti, to: (0, 0, 0)),
        ],
        out_specs=pl.BlockSpec((TILE, out_width), lambda i, ti, to: (i, 0)),
    )
    return pl.pallas_call(
        add_tiles_kernel,
        out_shape=jax.ShapeDtypeStruct(weight.shape, BF16),
        grid_spec=grid_spec,
        cost_estimate=pl.CostEstimate(flops=0, bytes_accessed=4 * depth * out_width, transcendentals=0),
        name="add_tiles",
    )(tile_in, tile_out, weight, tiles)


def tile_grad_kernel(in_ref, slot_ref, out_tile_ref, order_ref, *refs):
    o_ref = refs[-1]
    count = (len(refs) - 1) // 2
    total = jnp.zeros(o_ref.shape[1:], F32)
    for j in range(count):
        total += lax.dot_general(
            refs[j][0], refs[count + j][0, 0], (((0,), (0,)), ((), ())), preferred_element_type=F32
        )
    o_ref[0] = total


def tile_grads(halves, cot, tile_in, tile_slot, tile_out, order):
    rows = cot.shape[2]
    tiles = tile_in.shape[0]
    arrays, a_specs, c_specs = [], [], []
    for half in halves:
        for b in range(half.shape[0]):
            j = len(arrays)
            arrays.append(half)
            a_specs.append(pl.BlockSpec((1, rows, TILE), lambda t, ti, ts, to, od, b=b: (b, 0, ti[t])))
            c_specs.append(
                pl.BlockSpec((1, 1, rows, TILE), lambda t, ti, ts, to, od, j=j: (ts[t], od[j], 0, to[t]))
            )
    batches = len(arrays)
    grid_spec = pltpu.PrefetchScalarGridSpec(
        num_scalar_prefetch=4,
        grid=(tiles,),
        in_specs=a_specs + c_specs,
        out_specs=pl.BlockSpec((1, TILE, TILE), lambda t, ti, ts, to, od: (t, 0, 0)),
    )
    return pl.pallas_call(
        tile_grad_kernel,
        out_shape=jax.ShapeDtypeStruct((tiles, TILE, TILE), F32),
        grid_spec=grid_spec,
        compiler_params=pltpu.CompilerParams(vmem_limit_bytes=16 * 1024 * 1024),
        cost_estimate=pl.CostEstimate(
            flops=2 * tiles * batches * rows * TILE * TILE,
            bytes_accessed=4 * tiles * batches * rows * TILE,
            transcendentals=0,
        ),
        name="tile_gradient",
    )(tile_in, tile_slot, tile_out, order, *arrays, *([cot] * batches))


def up_grad_kernel(col_ref, low_ref, cot_ref, sum_ref, o_ref):
    o_ref[...] = sum_ref[...] + LOW_RANK_FACTOR * lax.dot_general(
        low_ref[...], cot_ref[0], (((0,), (0,)), ((), ())), preferred_element_type=F32
    )


def up_grad(col, low, cot, total):
    slots, length, segment = cot.shape
    rank = low.shape[1]
    grid_spec = pltpu.PrefetchScalarGridSpec(
        num_scalar_prefetch=1,
        grid=(slots,),
        in_specs=[
            pl.BlockSpec((length, rank), lambda k, c: (0, 0)),
            pl.BlockSpec((1, length, segment), lambda k, c: (k, 0, 0)),
            pl.BlockSpec((rank, segment), lambda k, c: (0, lax.rem(k + c[0], slots))),
        ],
        out_specs=pl.BlockSpec((rank, segment), lambda k, c: (0, lax.rem(k + c[0], slots))),
    )
    return pl.pallas_call(
        up_grad_kernel,
        out_shape=jax.ShapeDtypeStruct(total.shape, F32),
        grid_spec=grid_spec,
        input_output_aliases={3: 0},
        compiler_params=pltpu.CompilerParams(vmem_limit_bytes=24 * 1024 * 1024),
        cost_estimate=pl.CostEstimate(
            flops=2 * slots * length * segment * rank,
            bytes_accessed=2 * slots * length * segment,
            transcendentals=0,
        ),
        name="up_gradient",
    )(col[None], low, cot, total)


def swap(value, axis, bit, size):
    return lax.ppermute(value, axis, [(i, i ^ bit) for i in range(size)])


def row_bits(size):
    bits = []
    bit = size // 2
    while bit >= 1:
        bits.append(bit)
        bit //= 2
    return bits


def gather_row(value, size):
    pieces, slots = value, [0]
    halves = [pieces]
    for bit in row_bits(size):
        if len(halves) > 1:
            pieces = jnp.concatenate(halves, axis=0)
        halves = [pieces, swap(pieces, "row", bit, size)]
        slots = slots + [s ^ bit for s in slots]
    return halves, slots


def add_over_seq(value, size):
    if size == 2:
        return value + swap(value, "seq", 1, size)
    return lax.psum(value, "seq")


def hop(value, way, size, senders):
    pairs = [(i, i + 1) for i in senders if i + 1 < size]
    if way < 0:
        pairs = [(size - 1 - a, size - 1 - b) for a, b in pairs]
    return lax.ppermute(value, "col", pairs)


def by_slot(from_left, from_right, size):
    me = lax.axis_index("col")
    return [
        jnp.where(me + k < size, from_right[k - 1], from_left[size - 1 - k]) for k in range(1, size)
    ]


def target(way, t, size):
    me = lax.axis_index("col")
    last = size - 1
    return jnp.clip(last - t + me if way > 0 else t + me - last, 0, last)


def chunk_list(length, block):
    if length < 4 * block:
        return [(at, block) for at in range(0, length, block)]
    return [(0, block), (block, block)] + [(at, 2 * block) for at in range(2 * block, length, 2 * block)]


def low_rank_steps(partial, col, n_col, n_row):
    current = partial
    for bit in row_bits(n_col):
        half = current.shape[0] // 2
        upper = jnp.bitwise_and(col, bit) != 0
        keep = jnp.where(upper, current[half:], current[:half])
        give = jnp.where(upper, current[:half], current[half:])
        arrived = yield (lambda v, bit=bit: swap(v, "col", bit, n_col)), give.astype(BF16)
        current = keep + arrived.astype(F32)
    current = current.astype(BF16)
    for bit in reversed(row_bits(n_col)):
        arrived = yield (lambda v, bit=bit: swap(v, "col", bit, n_col)), current
        upper = jnp.bitwise_and(col, bit) != 0
        current = jnp.concatenate(
            [jnp.where(upper, arrived, current), jnp.where(upper, current, arrived)]
        )
    current = current[None]
    for bit in row_bits(n_row):
        arrived = yield (lambda v, bit=bit: swap(v, "row", bit, n_row)), current
        current = jnp.concatenate([current, arrived])
    yield "done", current


def tie(*values):
    return lax.optimization_barrier(values)


def local(
    queries,
    rotated_key_heads,
    value_head_states,
    document_index,
    output_projection_weight,
    frozen_down_factor,
    trained_up_factor,
    correction_tiles,
    tile_placement,
    cotangent,
):
    n_row, n_col, n_seq = lax.axis_size("row"), lax.axis_size("col"), lax.axis_size("seq")
    row, col, seq = lax.axis_index("row"), lax.axis_index("col"), lax.axis_index("seq")
    local_len, width = queries.shape[1], queries.shape[2]
    out_width = output_projection_weight.shape[1]
    segment = out_width // n_col
    seg_tiles = segment // TILE
    rank = frozen_down_factor.shape[1]
    block_rows = max(128, local_len // 4)
    chunks = chunk_list(local_len, block_rows)
    half_rows = n_row // 2
    ways = (1, -1)

    here = jnp.stack([rotated_key_heads[0], value_head_states[0]])
    if n_seq == 2:
        other = swap(here, "seq", 1, 2)
        both = jnp.concatenate([jnp.where(seq == 0, here, other), jnp.where(seq == 0, other, here)], axis=1)
    else:
        both = lax.all_gather(here, "seq", axis=1, tiled=True)
    keys, values_t = both[0], both[1].T
    key_block = min(256, keys.shape[0])
    documents = document_index[0]
    starts_all = jnp.searchsorted(documents, documents, side="left", method="compare_all").astype(jnp.int32)
    base = seq * local_len
    starts = lax.dynamic_slice_in_dim(starts_all, base, local_len, 0)
    block_at = jnp.arange(local_len // block_rows) * block_rows
    bounds = jnp.concatenate(
        [starts[block_at] // key_block, (base + block_at + block_rows - 1) // key_block + 1, base[None]]
    ).astype(jnp.int32)

    first_hop = {way: hop(cotangent, way, n_col, range(n_col)) for way in ways}

    gathered, low_parts = [], []
    for offset, rows in chunks:
        part = attend_chunk(
            queries[0], keys, values_t, bounds, starts[None], offset, rows, block_rows, key_block
        )
        low_parts.append(jnp.dot(part, frozen_down_factor, preferred_element_type=F32))
        halves, slots = gather_row(part[None], n_row)
        gathered.append(halves)
    order = jnp.bitwise_xor(row, jnp.array(slots, jnp.int32))

    coords = tile_placement.reshape(-1, 2)
    coords, bounds = tie(coords, bounds)
    tile_in, tile_out = coords[:, 0], coords[:, 1]
    weight = add_tiles(output_projection_weight, correction_tiles.reshape(-1, TILE, TILE), tile_in, tile_out)
    tile_slot = jnp.mod(tile_out // seg_tiles - col, n_col)
    tile_out = tile_out % seg_tiles

    inverse = jnp.array([slots.index(s) for s in range(n_row)], jnp.int32)
    batch_slot = inverse[jnp.bitwise_xor(row, jnp.arange(n_row))]

    jobs = []
    for q, (offset, rows) in enumerate(chunks):
        if rows == block_rows:
            jobs.append((q, 0, n_row, jnp.concatenate(gathered[q])))
        else:
            jobs.extend((q, h * half_rows, half_rows, gathered[q][h]) for h in range(2))
    jobs = [
        (q, lead, count, jnp.dot(part.reshape(count * chunks[q][1], width), weight, preferred_element_type=F32))
        for q, lead, count, part in jobs
    ]

    low_steps = low_rank_steps(jnp.concatenate(low_parts), col, n_col, n_row)
    low_next = next(low_steps)
    low_pending, low_done = None, None
    last = [{}, {}]
    got = [None] * len(jobs)
    streams = []
    for q, lead, count, _ in jobs:
        offset, rows = chunks[q]
        streams.append({way: [first_hop[way][lead:lead + count, offset:offset + rows]] for way in ways})
    for first in range(0, len(jobs), 2):
        for t in range(n_col - 1):
            for lane, at in enumerate(range(first, min(first + 2, len(jobs)))):
                q, lead, count, terms = jobs[at]
                sends = {}
                for way in ways:
                    send = lax.dynamic_slice_in_dim(terms, target(way, t, n_col) * segment, segment, 1)
                    if t > 0:
                        send = send + got[at][way].astype(F32)
                    send = send.astype(BF16)
                    if t + 1 < n_col - 1:
                        place = col if way > 0 else n_col - 1 - col
                        send = jnp.where(place <= t, send, streams[at][way][-1].reshape(send.shape))
                    sends[way] = send
                before = [last[lane][way] for way in ways] if last[lane] else []
                if low_pending is not None and lane == 1:
                    before = before + [low_pending]
                tied = tie(*[sends[way] for way in ways], *before)
                if low_pending is not None and lane == 1:
                    low_next = low_steps.send(tied[-1])
                    low_pending = None
                    if low_next[0] == "done":
                        low_done = low_next[1]
                        low_next = None
                arrived = {way: hop(tied[i], way, n_col, range(n_col)) for i, way in enumerate(ways)}
                if lane == 0 and low_next is not None and low_pending is None:
                    move, value = low_next
                    if before:
                        value, *_ = tie(value, *tied[len(ways):])
                    low_pending = move(value)
                last[lane] = arrived
                got[at] = arrived
                if t + 1 < n_col - 1:
                    for way in ways:
                        streams[at][way].append(
                            arrived[way].reshape(count, chunks[q][1], segment)
                        )
    while low_done is None:
        if low_pending is None:
            low_pending = low_next[0](low_next[1])
        low_next = low_steps.send(low_pending)
        low_pending = None
        if low_next[0] == "done":
            low_done = low_next[1]
    low = low_done
    low_ordered = low[batch_slot]

    up_here = lax.dynamic_slice_in_dim(trained_up_factor, col * segment, segment, 1)
    projected = jnp.zeros((n_row, local_len, segment), BF16)
    for at, (q, lead, count, terms) in enumerate(jobs):
        offset, rows = chunks[q]
        for j in range(count):
            low_term = jnp.dot(low[lead + j, offset:offset + rows], up_here, preferred_element_type=F32)
            mine = lax.dynamic_slice(terms, (j * rows, col * segment), (rows, segment))
            sums = mine + LOW_RANK_FACTOR * low_term
            for way in ways:
                sums = sums + got[at][way][j * rows:(j + 1) * rows].astype(F32)
            projected = lax.dynamic_update_slice(
                projected, sums.astype(BF16)[None], (order[lead + j], offset, 0)
            )

    tile_sum = jnp.zeros((coords.shape[0], TILE, TILE), F32)
    up_total = jnp.zeros((rank, out_width), F32)
    for q, (offset, rows) in enumerate(chunks):
        parts = []
        for at, job in enumerate(jobs):
            if job[0] == q:
                own = cotangent[job[1]:job[1] + job[2], offset:offset + rows]
                parts.append([own] + by_slot(streams[at][1], streams[at][-1], n_col))
        cot = jnp.concatenate(
            [jnp.concatenate([part[k] for part in parts])[None] for k in range(n_col)]
        )
        tile_sum = tile_sum + tile_grads(gathered[q], cot, tile_in, tile_slot, tile_out, order)
        up_total = up_grad(
            col,
            low_ordered[:, offset:offset + rows].reshape(n_row * rows, rank),
            cot.reshape(n_col, n_row * rows, segment),
            up_total,
        )

    up_gradient = add_over_seq(up_total, n_seq)
    tile_total = add_over_seq(tile_sum, n_seq)
    return projected, up_gradient, tile_total.reshape(correction_tiles.shape)


def solution(mesh):
    placed = (
        P("row", "seq", "col"),
        P("row", "seq", "col"),
        P("row", "seq", "col"),
        P("row", None),
        P("col", "row"),
        P("col", None),
        P(None, "row"),
        P("row", "col", None, None, None),
        P("row", "col", None, None),
        P(None, "seq", ("row", "col")),
    )
    return jax.shard_map(
        local,
        mesh=mesh,
        in_specs=placed,
        out_specs=(
            P(None, "seq", ("row", "col")),
            P(None, "row"),
            P("row", "col", None, None, None),
        ),
        check_vma=False,
    )
```

time: 1400 us -> 589 us (0.42)
  waiting for transfers between devices: 630 us -> 167 us
  blocking collectives: 281 us -> 0 us
  local copies, waits for them, and re-layouts: 208 us -> 36.6 us
  starting transfers between devices: 0.24 us -> 130 us
  matrix products: 177 us -> 75.7 us
  Pallas kernels: 0 us -> 78.9 us
    reduce_scatter x1 -> x0, waiting for transfers between devices: 331 us -> none  [local(): lax.psum_scatter(partial_value.reshape(sequence_rows, local_len, out_widt...]
    psum x1 -> x0, blocking collectives: 281 us -> none  [local(): low_rank_inner = lax.psum(low_rank_piece, 'col').astype(jnp.bfloat16)]
    all_gather x4 -> x0, waiting for transfers between devices: 233 us -> none  [the longest x1 104 us: local(): cot_full = lax.all_gather(cotangent, 'col', axis=2, tiled=True)]
    ppermute x0 -> x41, waiting for transfers between devices: none -> 167 us  [the longest x26 117 us: hop(): return lax.ppermute(value, 'col', pairs)]
    ppermute x0 -> x41, starting transfers between devices: none -> 130 us  [the longest x26 74.8 us: hop(): return lax.ppermute(value, 'col', pairs)]
    dot_general x10 -> x19, matrix products: 177 us -> 75.7 us  [the longest x4 49.2 us: local(): jnp.dot(part.reshape(count * chunks[q][1], width), weight, preferred_elem...]
    another operation x4 -> x0, local copies, waits for them, and re-layouts: 87.4 us -> none  [the longest x1 35.5 us: local(): partial_value.reshape(sequence_rows, local_len, out_width)]
    pallas_call x0 -> x10, Pallas kernels: none -> 78.9 us  [the longest x3 46.7 us: attend_chunk(): pl.pallas_call(functools.partial(attend_kernel, heads=heads, key_block=ke...]
  transfers between devices with their start and end apart: 6 -> 41, of which waited for: 6 -> 17; matrix products, arithmetic and copies ran while one was open for 21% -> 31% of each run, Pallas kernels for 0% -> 14%
where the time goes in v1:
time: 589 us; the launch traced here: 579 us
  waiting for transfers between devices  167 us (28%)
  starting transfers between devices  130 us (22%)
  other arithmetic  80.7 us (14%)
  Pallas kernels  78.9 us (13%)
  matrix products  75.7 us (13%)
  local copies, waits for them, and re-layouts  36.6 us (6%)
  between operations  10.2 us (2%)
    ppermute x26, waiting for transfers between devices, hop(): return lax.ppermute(value, 'col', pairs)  117 us
    ppermute x26, starting transfers between devices, hop(): return lax.ppermute(value, 'col', pairs)  74.8 us
    ppermute x15, starting transfers between devices, swap(): return lax.ppermute(value, axis, [(i, i ^ bit) for i in range(size)])  55.6 us
    ppermute x15, waiting for transfers between devices, swap(): return lax.ppermute(value, axis, [(i, i ^ bit) for i in range(size)])  49.3 us
    dot_general x4, matrix products, local(): jnp.dot(part.reshape(count * chunks[q][1], width), weight, preferred_elem...  49.2 us
    pallas_call x3, Pallas kernels, attend_chunk(): pl.pallas_call(functools.partial(attend_kernel, heads=heads, key_block=ke...  46.7 us
    select_n x8, other arithmetic, local(): send = jnp.where(place <= t, send, streams[at][way][-1].reshape(send.shape))  25.4 us
    dot_general x12, matrix products, local(): jnp.dot(low[lead + j, offset:offset + rows], up_here, preferred_element_t...  19.2 us
  transfers between devices with their start and end apart: 41, of which 17 were waited for; matrix products, arithmetic and copies ran while one was open for 31% of the time, Pallas kernels for 14%

profile of v1, /device:TPU:0, one launch (start us, length us, event | category | flops | bytes accessed | tf_op | source)
XLA Modules:
  0.0 579.2 jit_solution(10778590306324033555)
XLA Ops:
  2.1 7.5 %collective-permute-start.5 = (bf16[4,1024,512]{2,1,0:T(8,128)(2,1)}, bf16[4,1024,512]{2,1,0:T(8,128)(2,1)}, u32[]{:S(2)}, u32[]{:S(2)}) collective-permute-start(bf16[4,1024,512]{2,1,0:T(8,128)(2,1)} %param.21), channel_id=1, source_target_pairs={{0,2},{2,4},{4,6},{1,3},{3,5},{5,7},{8,10},{10,12},{12,14},{9,11},... | collective-permute-start | bytes 12582920 | tf_op jit(solution)/shard_map/ppermute | solution.py:238
  21.7 15.3 %collective-permute-done = bf16[2,1024,256]{1,2,0:T(8,128)(2,1)} collective-permute-done((bf16[2,1024,256]{1,2,0:T(8,128)(2,1)S(1)}, bf16[2,1024,256]{1,2,0:T(8,128)(2,1)}, u32[]{:S(2)}, u32[]{:S(2)}) %collective-permute-start) | collective-permute-done | bytes 1048608 | tf_op jit(solution)/shard_map/ppermute | solution.py:205
  44.1 7.5 %attention.3 = bf16[256,2048]{1,0:T(8,128)(2,1)S(1)} custom-call(s32[9]{0:T(128)S(1)} %pad_add_fusion.bounds_ref, bf16[1024,2048]{1,0:T(8,128)(2,1)S(1)} %bitcast.213, bf16[2048,256]{1,0:T(8,128)(2,1)S(1)} %copy.30.k_ref, bf16[256,2048]{1,0:T(8,128)(2,1)S(1)} %get-tuple-element.117.vt_ref, s32[1,1024]{1,0:T(1,128)S(1)} %bitcast.202), custom_call_target="tpu_custom_call" | custom-call | flops 2863300608 | bytes 2097152 | tf_op jit(solution)/shard_map/attention/pallas_call | solution.py:82
  55.7 25.7 %attention.4 = bf16[512,2048]{1,0:T(8,128)(2,1)} custom-call(s32[9]{0:T(128)S(1)} %pad_add_fusion.bounds_ref, bf16[1024,2048]{1,0:T(8,128)(2,1)S(1)} %bitcast.214, bf16[2048,256]{1,0:T(8,128)(2,1)S(1)} %copy.30.k_ref, bf16[256,2048]{1,0:T(8,128)(2,1)S(1)} %get-tuple-element.117.vt_ref, s32[1,1024]{1,0:T(1,128)S(1)} %bitcast.203), custom_call_target="tpu_custom_call" | custom-call | flops 5726617600 | bytes 4194304 | tf_op jit(solution)/shard_map/attention/pallas_call | solution.py:82
  81.4 5.7 collective-permute-start.3
  87.4 8.6 %collective-permute-start.2 = (bf16[2,256,2048]{2,1,0:T(8,128)(2,1)S(1)}, bf16[2,256,2048]{2,1,0:T(8,128)(2,1)}, u32[]{:S(2)}, u32[]{:S(2)}) collective-permute-start(bf16[2,256,2048]{2,1,0:T(8,128)(2,1)S(1)} %pad_maximum_fusion.9.refs_0_.refs_1_), channel_id=1, source_target_pairs={{0,8},{8,0},{16,24},{24,16},{1,9},{9,1},{17,25},{25,17},{2,10},{10... | collective-permute-start | bytes 6291464 | tf_op jit(solution)/shard_map/ppermute | solution.py:205
  96.0 13.5 %attention.5 = bf16[256,2048]{1,0:T(8,128)(2,1)} custom-call(s32[9]{0:T(128)S(1)} %pad_add_fusion.bounds_ref, bf16[1024,2048]{1,0:T(8,128)(2,1)S(1)} %bitcast.215, bf16[2048,256]{1,0:T(8,128)(2,1)S(1)} %copy-done.10, bf16[256,2048]{1,0:T(8,128)(2,1)S(1)} %copy-done.12, s32[1,1024]{1,0:T(1,128)S(1)} %bitcast.204), custom_call_target="tpu_custom_call" | custom-call | flops 2863300608 | bytes 2097152 | tf_op jit(solution)/shard_map/attention/pallas_call | solution.py:82
  119.8 12.9 %add_tiles.1 = bf16[2048,2048]{1,0:T(8,128)(2,1)} custom-call(s32[5]{0:T(128)} %get-tuple-element.126.in_ref, s32[5]{0:T(128)} %get-tuple-element.125.out_tile_ref, bf16[2048,2048]{1,0:T(8,128)(2,1)} %w_ref.1, bf16[5,128,128]{2,1,0:T(8,128)(2,1)} %bitcast.250), custom_call_target="tpu_custom_call" | custom-call | bytes 16777216 | tf_op jit(solution)/shard_map/add_tiles/pallas_call | solution.py:117
  140.6 7.5 %collective-permute-done.7 = bf16[1,256,2048]{2,1,0:T(8,128)(2,1)} collective-permute-done((bf16[1,256,2048]{2,1,0:T(8,128)(2,1)}, bf16[1,256,2048]{2,1,0:T(8,128)(2,1)}, u32[]{:S(2)}, u32[]{:S(2)}) %collective-permute-start.7) | collective-permute-done | bytes 1048608 | tf_op jit(solution)/shard_map/ppermute | solution.py:205
  152.9 7.8 %collective-permute-start.8 = (bf16[2,256,2048]{2,1,0:T(8,128)(2,1)S(1)}, bf16[2,256,2048]{2,1,0:T(8,128)(2,1)S(1)}, u32[]{:S(2)}, u32[]{:S(2)}) collective-permute-start(bf16[2,256,2048]{2,1,0:T(8,128)(2,1)S(1)} %pad_maximum_fusion.10.refs_0_.refs_1_), channel_id=1, source_target_pairs={{0,8},{8,0},{16,24},{24,16},{1,9},{9,1},{17,25},{25,17},{2,10},{10... | collective-permute-start | bytes 6291464 | tf_op jit(solution)/shard_map/ppermute | solution.py:205
  167.4 11.4 %fusion.71 = f32[1024,2048]{1,0:T(8,128)S(1)} fusion(bf16[1024,2048]{1,0:T(8,128)(2,1)S(1)} %bitcast.241, bf16[2048,2048]{1,0:T(8,128)(2,1)} %add_tiles.1), kind=kOutput, calls=%fused_computation.203 | convolution fusion | flops 8589934592 | bytes 20971520 | tf_op jit(solution)/shard_map/dot_general | solution.py:357
  185.5 11.2 %fusion.76 = f32[1024,2048]{1,0:T(8,128)S(1)} fusion(bf16[1024,2048]{1,0:T(8,128)(2,1)S(1)} %bitcast.205, bf16[2048,2048]{1,0:T(8,128)(2,1)} %add_tiles.1), kind=kOutput, calls=%fused_computation.208 | convolution fusion | flops 8589934592 | bytes 20971520 | tf_op jit(solution)/shard_map/dot_general | solution.py:357
  200.1 6.9 %collective-permute-done.19 = bf16[1024,512]{1,0:T(8,128)(2,1)S(1)} collective-permute-done((bf16[1024,512]{1,0:T(8,128)(2,1)S(1)}, bf16[1024,512]{1,0:T(8,128)(2,1)S(1)}, u32[]{:S(2)}, u32[]{:S(2)}) %collective-permute-start.19) | collective-permute-done | bytes 1048608 | tf_op jit(solution)/shard_map/ppermute | solution.py:238
  207.0 4.3 collective-permute-done.20
  211.3 5.1 fusion.3
  220.6 13.2 %fusion.73 = f32[1024,2048]{1,0:T(8,128)} fusion(bf16[1024,2048]{1,0:T(8,128)(2,1)S(1)} %bitcast.240, bf16[2048,2048]{1,0:T(8,128)(2,1)} %add_tiles.1), kind=kOutput, calls=%fused_computation.205 | convolution fusion | flops 8589934592 | bytes 20971520 | tf_op jit(solution)/shard_map/dot_general | solution.py:357
  260.0 4.6 collective-permute-start.10
  267.7 4.3 tile_gradient.3
  274.4 19.9 %collective-permute-done.10 = bf16[1024,512]{1,0:T(8,128)(2,1)S(1)} collective-permute-done((bf16[1024,512]{1,0:T(8,128)(2,1)S(1)}, bf16[1024,512]{1,0:T(8,128)(2,1)S(1)}, u32[]{:S(2)}, u32[]{:S(2)}) %collective-permute-start.10) | collective-permute-done | bytes 1048608 | tf_op jit(solution)/shard_map/ppermute | solution.py:238
  309.4 4.6 collective-permute-start.31
  315.4 13.4 %fusion.72 = f32[1024,2048]{1,0:T(8,128)} fusion(bf16[1024,2048]{1,0:T(8,128)(2,1)S(1)} %bitcast.206, bf16[2048,2048]{1,0:T(8,128)(2,1)} %add_tiles.1), kind=kOutput, calls=%fused_computation.204 | convolution fusion | flops 8589934592 | bytes 20971520 | tf_op jit(solution)/shard_map/dot_general | solution.py:357
  328.8 21.3 %collective-permute-done.31 = bf16[1024,512]{1,0:T(8,128)(2,1)S(1)} collective-permute-done((bf16[1024,512]{1,0:T(8,128)(2,1)}, bf16[1024,512]{1,0:T(8,128)(2,1)S(1)}, u32[]{:S(2)}, u32[]{:S(2)}) %collective-permute-start.31) | collective-permute-done | bytes 1048608 | tf_op jit(solution)/shard_map/ppermute | solution.py:238
  354.2 4.8 fusion.7
  362.2 4.6 collective-permute-start.33
  373.1 16.8 %collective-permute-done.34 = bf16[1024,512]{1,0:T(8,128)(2,1)S(1)} collective-permute-done((bf16[1024,512]{1,0:T(8,128)(2,1)S(1)}, bf16[1024,512]{1,0:T(8,128)(2,1)S(1)}, u32[]{:S(2)}, u32[]{:S(2)}) %collective-permute-start.34) | collective-permute-done | bytes 1048608 | tf_op jit(solution)/shard_map/ppermute | solution.py:238
  397.9 15.1 %collective-permute-done.16 = bf16[1024,512]{1,0:T(8,128)(2,1)S(1)} collective-permute-done((bf16[1024,512]{1,0:T(8,128)(2,1)}, bf16[1024,512]{1,0:T(8,128)(2,1)S(1)}, u32[]{:S(2)}, u32[]{:S(2)}) %collective-permute-start.16) | collective-permute-done | bytes 1048608 | tf_op jit(solution)/shard_map/ppermute | solution.py:238
  413.0 8.9 %collective-permute-start.25 = (bf16[1024,512]{1,0:T(8,128)(2,1)}, bf16[1024,512]{1,0:T(8,128)(2,1)S(1)}, u32[]{:S(2)}, u32[]{:S(2)}) collective-permute-start(bf16[1024,512]{1,0:T(8,128)(2,1)} %get-tuple-element.51), channel_id=1, source_target_pairs={{0,2},{2,4},{4,6},{1,3},{3,5},{5,7},{8,10},{10,12},{12,14},{9,11},... | collective-permute-start | bytes 3145736 | tf_op jit(solution)/shard_map/ppermute | solution.py:238
  431.5 6.9 %collective-permute-done.25 = bf16[1024,512]{1,0:T(8,128)(2,1)S(1)} collective-permute-done((bf16[1024,512]{1,0:T(8,128)(2,1)}, bf16[1024,512]{1,0:T(8,128)(2,1)S(1)}, u32[]{:S(2)}, u32[]{:S(2)}) %collective-permute-start.25) | collective-permute-done | bytes 1048608 | tf_op jit(solution)/shard_map/ppermute | solution.py:238
  454.4 5.7 collective-permute-start.35
  467.0 5.1 collective-permute-done.28
  506.3 19.8 %collective-permute-start.39 = (f32[256,2048]{1,0:T(8,128)S(1)}, f32[256,2048]{1,0:T(8,128)S(1)}, u32[]{:S(2)}, u32[]{:S(2)}) collective-permute-start(f32[256,2048]{1,0:T(8,128)S(1)} %up_gradient.5), channel_id=1, source_target_pairs={{0,1},{1,0},{2,3},{3,2},{4,5},{5,4},{6,7},{7,6},{8,9},{9,8},{10,11... | collective-permute-start | bytes 6291464 | tf_op jit(solution)/shard_map/ppermute | solution.py:205
  545.9 26.4 %collective-permute-done.40 = f32[5,128,128]{2,1,0:T(8,128)S(1)} collective-permute-done((f32[5,128,128]{2,1,0:T(8,128)S(1)}, f32[5,128,128]{2,1,0:T(8,128)S(1)}, u32[]{:S(2)}, u32[]{:S(2)}) %collective-permute-start.40) | collective-permute-done | bytes 327712 | tf_op jit(solution)/shard_map/ppermute | solution.py:205
  (293 shorter events, 222.6 us)
Async XLA Ops:
  0.7 162.6 %collective-permute-start.6 = (bf16[4,1024,512]{2,1,0:T(8,128)(2,1)}, bf16[4,1024,512]{2,1,0:T(8,128)(2,1)}, u32[]{:S(2)}, u32[]{:S(2)}) collective-permute-start(bf16[4,1024,512]{2,1,0:T(8,128)(2,1)} %param.21), channel_id=1, source_target_pairs={{6,4},{4,2},{2,0},{7,5},{5,3},{3,1},{14,12},{12,10},{10,8},{15,13}... | collective-permute-start | bytes 12582920 | tf_op jit(solution)/shard_map/ppermute | solution.py:238
  2.1 176.7 %collective-permute-start.5 = (bf16[4,1024,512]{2,1,0:T(8,128)(2,1)}, bf16[4,1024,512]{2,1,0:T(8,128)(2,1)}, u32[]{:S(2)}, u32[]{:S(2)}) collective-permute-start(bf16[4,1024,512]{2,1,0:T(8,128)(2,1)} %param.21), channel_id=1, source_target_pairs={{0,2},{2,4},{4,6},{1,3},{3,5},{5,7},{8,10},{10,12},{12,14},{9,11},... | collective-permute-start | bytes 12582920 | tf_op jit(solution)/shard_map/ppermute | solution.py:238
  51.6 35.6 %collective-permute-start.1 = (bf16[1,256,2048]{2,1,0:T(8,128)(2,1)S(1)}, bf16[1,256,2048]{2,1,0:T(8,128)(2,1)S(1)}, u32[]{:S(2)}, u32[]{:S(2)}) collective-permute-start(bf16[1,256,2048]{2,1,0:T(8,128)(2,1)S(1)} %bitcast.207), channel_id=1, source_target_pairs={{0,16},{8,24},{16,0},{24,8},{1,17},{9,25},{17,1},{25,9},{2,18},{10... | collective-permute-start | bytes 3145736 | tf_op jit(solution)/shard_map/ppermute | solution.py:205
  81.4 71.5 %collective-permute-start.3 = (bf16[1,512,2048]{2,1,0:T(8,128)(2,1)}, bf16[1,512,2048]{2,1,0:T(8,128)(2,1)}, u32[]{:S(2)}, u32[]{:S(2)}) collective-permute-start(bf16[1,512,2048]{2,1,0:T(8,128)(2,1)} %bitcast.15), channel_id=1, source_target_pairs={{0,16},{8,24},{16,0},{24,8},{1,17},{9,25},{17,1},{25,9},{2,18},{10... | collective-permute-start | bytes 6291464 | tf_op jit(solution)/shard_map/ppermute | solution.py:205
  87.4 78.2 %collective-permute-start.2 = (bf16[2,256,2048]{2,1,0:T(8,128)(2,1)S(1)}, bf16[2,256,2048]{2,1,0:T(8,128)(2,1)}, u32[]{:S(2)}, u32[]{:S(2)}) collective-permute-start(bf16[2,256,2048]{2,1,0:T(8,128)(2,1)S(1)} %pad_maximum_fusion.9.refs_0_.refs_1_), channel_id=1, source_target_pairs={{0,8},{8,0},{16,24},{24,16},{1,9},{9,1},{17,25},{25,17},{2,10},{10... | collective-permute-start | bytes 6291464 | tf_op jit(solution)/shard_map/ppermute | solution.py:205
  109.5 38.6 %collective-permute-start.7 = (bf16[1,256,2048]{2,1,0:T(8,128)(2,1)}, bf16[1,256,2048]{2,1,0:T(8,128)(2,1)}, u32[]{:S(2)}, u32[]{:S(2)}) collective-permute-start(bf16[1,256,2048]{2,1,0:T(8,128)(2,1)} %bitcast.19), channel_id=1, source_target_pairs={{0,16},{8,24},{16,0},{24,8},{1,17},{9,25},{17,1},{25,9},{2,18},{10... | collective-permute-start | bytes 3145736 | tf_op jit(solution)/shard_map/ppermute | solution.py:205
  148.1 111.9 %collective-permute-start.9 = (bf16[512,256]{1,0:T(8,128)(2,1)}, bf16[512,256]{1,0:T(8,128)(2,1)}, u32[]{:S(2)}, u32[]{:S(2)}) collective-permute-start(bf16[512,256]{1,0:T(8,128)(2,1)} %get-tuple-element.131), channel_id=1, source_target_pairs={{0,4},{2,6},{4,0},{6,2},{1,5},{3,7},{5,1},{7,3},{8,12},{10,14},{12... | collective-permute-start | bytes 786440 | tf_op jit(solution)/shard_map/ppermute | solution.py:205
  152.9 43.8 %collective-permute-start.8 = (bf16[2,256,2048]{2,1,0:T(8,128)(2,1)S(1)}, bf16[2,256,2048]{2,1,0:T(8,128)(2,1)S(1)}, u32[]{:S(2)}, u32[]{:S(2)}) collective-permute-start(bf16[2,256,2048]{2,1,0:T(8,128)(2,1)S(1)} %pad_maximum_fusion.10.refs_0_.refs_1_), channel_id=1, source_target_pairs={{0,8},{8,0},{16,24},{24,16},{1,9},{9,1},{17,25},{25,17},{2,10},{10... | collective-permute-start | bytes 6291464 | tf_op jit(solution)/shard_map/ppermute | solution.py:205
  163.3 150.8 %collective-permute-start.4 = (bf16[2,512,2048]{2,1,0:T(8,128)(2,1)S(1)}, bf16[2,512,2048]{2,1,0:T(8,128)(2,1)S(1)}, u32[]{:S(2)}, u32[]{:S(2)}) collective-permute-start(bf16[2,512,2048]{2,1,0:T(8,128)(2,1)S(1)} %pad_maximum_fusion.3.refs_0_.refs_1_), channel_id=1, source_target_pairs={{0,8},{8,0},{16,24},{24,16},{1,9},{9,1},{17,25},{25,17},{2,10},{10... | collective-permute-start | bytes 12582920 | tf_op jit(solution)/shard_map/ppermute | solution.py:205
  184.1 27.1 %collective-permute-start.20 = (bf16[1024,512]{1,0:T(8,128)(2,1)S(1)}, bf16[1024,512]{1,0:T(8,128)(2,1)}, u32[]{:S(2)}, u32[]{:S(2)}) collective-permute-start(bf16[1024,512]{1,0:T(8,128)(2,1)S(1)} %get-tuple-element.46), channel_id=1, source_target_pairs={{6,4},{4,2},{2,0},{7,5},{5,3},{3,1},{14,12},{12,10},{10,8},{15,13}... | collective-permute-start | bytes 3145736 | tf_op jit(solution)/shard_map/ppermute | solution.py:238
  219.3 26.1 %collective-permute-start.22 = (bf16[1024,512]{1,0:T(8,128)(2,1)}, bf16[1024,512]{1,0:T(8,128)(2,1)S(1)}, u32[]{:S(2)}, u32[]{:S(2)}) collective-permute-start(bf16[1024,512]{1,0:T(8,128)(2,1)} %get-tuple-element.48), channel_id=1, source_target_pairs={{6,4},{4,2},{2,0},{7,5},{5,3},{3,1},{14,12},{12,10},{10,8},{15,13}... | collective-permute-start | bytes 3145736 | tf_op jit(solution)/shard_map/ppermute | solution.py:238
  248.5 59.6 %collective-permute-start.23 = (bf16[1024,512]{1,0:T(8,128)(2,1)S(1)}, bf16[1024,512]{1,0:T(8,128)(2,1)}, u32[]{:S(2)}, u32[]{:S(2)}) collective-permute-start(bf16[1024,512]{1,0:T(8,128)(2,1)S(1)} %get-tuple-element.49), channel_id=1, source_target_pairs={{0,2},{2,4},{4,6},{1,3},{3,5},{5,7},{8,10},{10,12},{12,14},{9,11},... | collective-permute-start | bytes 3145736 | tf_op jit(solution)/shard_map/ppermute | solution.py:238
  251.9 57.5 %collective-permute-start.24 = (bf16[1024,512]{1,0:T(8,128)(2,1)S(1)}, bf16[1024,512]{1,0:T(8,128)(2,1)}, u32[]{:S(2)}, u32[]{:S(2)}) collective-permute-start(bf16[1024,512]{1,0:T(8,128)(2,1)S(1)} %get-tuple-element.50), channel_id=1, source_target_pairs={{6,4},{4,2},{2,0},{7,5},{5,3},{3,1},{14,12},{12,10},{10,8},{15,13}... | collective-permute-start | bytes 3145736 | tf_op jit(solution)/shard_map/ppermute | solution.py:238
  260.0 34.3 %collective-permute-start.10 = (bf16[1024,512]{1,0:T(8,128)(2,1)S(1)}, bf16[1024,512]{1,0:T(8,128)(2,1)S(1)}, u32[]{:S(2)}, u32[]{:S(2)}) collective-permute-start(bf16[1024,512]{1,0:T(8,128)(2,1)S(1)} %get-tuple-element.35), channel_id=1, source_target_pairs={{0,2},{2,4},{4,6},{1,3},{3,5},{5,7},{8,10},{10,12},{12,14},{9,11},... | collective-permute-start | bytes 3145736 | tf_op jit(solution)/shard_map/ppermute | solution.py:238
  264.7 36.2 %collective-permute-start.11 = (bf16[1024,512]{1,0:T(8,128)(2,1)S(1)}, bf16[1024,512]{1,0:T(8,128)(2,1)S(1)}, u32[]{:S(2)}, u32[]{:S(2)}) collective-permute-start(bf16[1024,512]{1,0:T(8,128)(2,1)S(1)} %get-tuple-element.36), channel_id=1, source_target_pairs={{6,4},{4,2},{2,0},{7,5},{5,3},{3,1},{14,12},{12,10},{10,8},{15,13}... | collective-permute-start | bytes 3145736 | tf_op jit(solution)/shard_map/ppermute | solution.py:238
  304.1 58.1 %collective-permute-start.15 = (bf16[256,256]{1,0:T(8,128)(2,1)S(1)}, bf16[256,256]{1,0:T(8,128)(2,1)S(1)}, u32[]{:S(2)}, u32[]{:S(2)}) collective-permute-start(bf16[256,256]{1,0:T(8,128)(2,1)S(1)} %add_convert_fusion.28), channel_id=1, source_target_pairs={{0,2},{2,0},{4,6},{6,4},{1,3},{3,1},{5,7},{7,5},{8,10},{10,8},{12,... | collective-permute-start | bytes 393224 | tf_op jit(solution)/shard_map/ppermute | solution.py:205
  304.1 56.2 %collective-permute-start.13 = (bf16[1024,512]{1,0:T(8,128)(2,1)S(1)}, bf16[1024,512]{1,0:T(8,128)(2,1)S(1)}, u32[]{:S(2)}, u32[]{:S(2)}) collective-permute-start(bf16[1024,512]{1,0:T(8,128)(2,1)S(1)} %get-tuple-element.38), channel_id=1, source_target_pairs={{0,2},{2,4},{4,6},{1,3},{3,5},{5,7},{8,10},{10,12},{12,14},{9,11},... | collective-permute-start | bytes 3145736 | tf_op jit(solution)/shard_map/ppermute | solution.py:238
  308.1 52.2 %collective-permute-start.14 = (bf16[1024,512]{1,0:T(8,128)(2,1)S(1)}, bf16[1024,512]{1,0:T(8,128)(2,1)S(1)}, u32[]{:S(2)}, u32[]{:S(2)}) collective-permute-start(bf16[1024,512]{1,0:T(8,128)(2,1)S(1)} %get-tuple-element.39), channel_id=1, source_target_pairs={{6,4},{4,2},{2,0},{7,5},{5,3},{3,1},{14,12},{12,10},{10,8},{15,13}... | collective-permute-start | bytes 3145736 | tf_op jit(solution)/shard_map/ppermute | solution.py:238
  309.4 40.6 %collective-permute-start.31 = (bf16[1024,512]{1,0:T(8,128)(2,1)}, bf16[1024,512]{1,0:T(8,128)(2,1)S(1)}, u32[]{:S(2)}, u32[]{:S(2)}) collective-permute-start(bf16[1024,512]{1,0:T(8,128)(2,1)} %get-tuple-element.57), channel_id=1, source_target_pairs={{0,2},{2,4},{4,6},{1,3},{3,5},{5,7},{8,10},{10,12},{12,14},{9,11},... | collective-permute-start | bytes 3145736 | tf_op jit(solution)/shard_map/ppermute | solution.py:238
  314.1 40.1 %collective-permute-start.32 = (bf16[1024,512]{1,0:T(8,128)(2,1)}, bf16[1024,512]{1,0:T(8,128)(2,1)}, u32[]{:S(2)}, u32[]{:S(2)}) collective-permute-start(bf16[1024,512]{1,0:T(8,128)(2,1)} %get-tuple-element.58), channel_id=1, source_target_pairs={{6,4},{4,2},{2,0},{7,5},{5,3},{3,1},{14,12},{12,10},{10,8},{15,13}... | collective-permute-start | bytes 3145736 | tf_op jit(solution)/shard_map/ppermute | solution.py:238
  359.0 30.9 %collective-permute-start.34 = (bf16[1024,512]{1,0:T(8,128)(2,1)S(1)}, bf16[1024,512]{1,0:T(8,128)(2,1)S(1)}, u32[]{:S(2)}, u32[]{:S(2)}) collective-permute-start(bf16[1024,512]{1,0:T(8,128)(2,1)S(1)} %get-tuple-element.60), channel_id=1, source_target_pairs={{6,4},{4,2},{2,0},{7,5},{5,3},{3,1},{14,12},{12,10},{10,8},{15,13}... | collective-permute-start | bytes 3145736 | tf_op jit(solution)/shard_map/ppermute | solution.py:238
  362.2 30.5 %collective-permute-start.33 = (bf16[1024,512]{1,0:T(8,128)(2,1)}, bf16[1024,512]{1,0:T(8,128)(2,1)S(1)}, u32[]{:S(2)}, u32[]{:S(2)}) collective-permute-start(bf16[1024,512]{1,0:T(8,128)(2,1)} %get-tuple-element.59), channel_id=1, source_target_pairs={{0,2},{2,4},{4,6},{1,3},{3,5},{5,7},{8,10},{10,12},{12,14},{9,11},... | collective-permute-start | bytes 3145736 | tf_op jit(solution)/shard_map/ppermute | solution.py:238
  366.9 31.0 %collective-permute-start.18 = (bf16[512,256]{1,0:T(8,128)(2,1)S(1)}, bf16[512,256]{1,0:T(8,128)(2,1)S(1)}, u32[]{:S(2)}, u32[]{:S(2)}) collective-permute-start(bf16[512,256]{1,0:T(8,128)(2,1)S(1)} %pad_maximum_fusion.19), channel_id=1, source_target_pairs={{0,4},{2,6},{4,0},{6,2},{1,5},{3,7},{5,1},{7,3},{8,12},{10,14},{12... | collective-permute-start | bytes 786440 | tf_op jit(solution)/shard_map/ppermute | solution.py:205
  367.0 46.0 %collective-permute-start.16 = (bf16[1024,512]{1,0:T(8,128)(2,1)}, bf16[1024,512]{1,0:T(8,128)(2,1)S(1)}, u32[]{:S(2)}, u32[]{:S(2)}) collective-permute-start(bf16[1024,512]{1,0:T(8,128)(2,1)} %get-tuple-element.41), channel_id=1, source_target_pairs={{0,2},{2,4},{4,6},{1,3},{3,5},{5,7},{8,10},{10,12},{12,14},{9,11},... | collective-permute-start | bytes 3145736 | tf_op jit(solution)/shard_map/ppermute | solution.py:238
  368.9 44.1 %collective-permute-start.17 = (bf16[1024,512]{1,0:T(8,128)(2,1)S(1)}, bf16[1024,512]{1,0:T(8,128)(2,1)S(1)}, u32[]{:S(2)}, u32[]{:S(2)}) collective-permute-start(bf16[1024,512]{1,0:T(8,128)(2,1)S(1)} %get-tuple-element.42), channel_id=1, source_target_pairs={{6,4},{4,2},{2,0},{7,5},{5,3},{3,1},{14,12},{12,10},{10,8},{15,13}... | collective-permute-start | bytes 3145736 | tf_op jit(solution)/shard_map/ppermute | solution.py:238
  452.1 25.4 %collective-permute-start.30 = (bf16[2,1024,256]{2,1,0:T(8,128)(2,1)S(1)}, bf16[2,1024,256]{2,1,0:T(8,128)(2,1)S(1)}, u32[]{:S(2)}, u32[]{:S(2)}) collective-permute-start(bf16[2,1024,256]{2,1,0:T(8,128)(2,1)S(1)} %pad_maximum_fusion.17), channel_id=1, source_target_pairs={{0,8},{8,0},{16,24},{24,16},{1,9},{9,1},{17,25},{25,17},{2,10},{10... | collective-permute-start | bytes 3145736 | tf_op jit(solution)/shard_map/ppermute | solution.py:205
  454.4 87.5 %collective-permute-start.35 = (bf16[1024,512]{1,0:T(8,128)(2,1)}, bf16[1024,512]{1,0:T(8,128)(2,1)}, u32[]{:S(2)}, u32[]{:S(2)}) collective-permute-start(bf16[1024,512]{1,0:T(8,128)(2,1)} %get-tuple-element.61), channel_id=1, source_target_pairs={{0,2},{2,4},{4,6},{1,3},{3,5},{5,7},{8,10},{10,12},{12,14},{9,11},... | collective-permute-start | bytes 3145736 | tf_op jit(solution)/shard_map/ppermute | solution.py:238
  460.1 81.9 %collective-permute-start.36 = (bf16[1024,512]{1,0:T(8,128)(2,1)}, bf16[1024,512]{1,0:T(8,128)(2,1)}, u32[]{:S(2)}, u32[]{:S(2)}) collective-permute-start(bf16[1024,512]{1,0:T(8,128)(2,1)} %get-tuple-element.62), channel_id=1, source_target_pairs={{6,4},{4,2},{2,0},{7,5},{5,3},{3,1},{14,12},{12,10},{10,8},{15,13}... | collective-permute-start | bytes 3145736 | tf_op jit(solution)/shard_map/ppermute | solution.py:238
  486.7 86.4 %collective-permute-start.37 = (bf16[1024,512]{1,0:T(8,128)(2,1)S(1)}, bf16[1024,512]{1,0:T(8,128)(2,1)S(1)}, u32[]{:S(2)}, u32[]{:S(2)}) collective-permute-start(bf16[1024,512]{1,0:T(8,128)(2,1)S(1)} %copy-done.46), channel_id=1, source_target_pairs={{0,2},{2,4},{4,6},{1,3},{3,5},{5,7},{8,10},{10,12},{12,14},{9,11},... | collective-permute-start | bytes 3145736 | tf_op jit(solution)/shard_map/ppermute | solution.py:238
  490.4 82.7 %collective-permute-start.38 = (bf16[1024,512]{1,0:T(8,128)(2,1)S(1)}, bf16[1024,512]{1,0:T(8,128)(2,1)S(1)}, u32[]{:S(2)}, u32[]{:S(2)}) collective-permute-start(bf16[1024,512]{1,0:T(8,128)(2,1)S(1)} %copy-done.45), channel_id=1, source_target_pairs={{6,4},{4,2},{2,0},{7,5},{5,3},{3,1},{14,12},{12,10},{10,8},{15,13}... | collective-permute-start | bytes 3145736 | tf_op jit(solution)/shard_map/ppermute | solution.py:238
  506.3 70.0 %collective-permute-start.39 = (f32[256,2048]{1,0:T(8,128)S(1)}, f32[256,2048]{1,0:T(8,128)S(1)}, u32[]{:S(2)}, u32[]{:S(2)}) collective-permute-start(f32[256,2048]{1,0:T(8,128)S(1)} %up_gradient.5), channel_id=1, source_target_pairs={{0,1},{1,0},{2,3},{3,2},{4,5},{5,4},{6,7},{7,6},{8,9},{9,8},{10,11... | collective-permute-start | bytes 6291464 | tf_op jit(solution)/shard_map/ppermute | solution.py:205
  541.9 30.4 %collective-permute-start.40 = (f32[5,128,128]{2,1,0:T(8,128)S(1)}, f32[5,128,128]{2,1,0:T(8,128)S(1)}, u32[]{:S(2)}, u32[]{:S(2)}) collective-permute-start(f32[5,128,128]{2,1,0:T(8,128)S(1)} %add_add_fusion), channel_id=1, source_target_pairs={{0,1},{1,0},{2,3},{3,2},{4,5},{5,4},{6,7},{7,6},{8,9},{9,8},{10,11... | collective-permute-start | bytes 983048 | tf_op jit(solution)/shard_map/ppermute | solution.py:205
  (75 other events, 1641.2 us)

commit v2 on v1

--- a/solution.py
+++ b/solution.py
@@ -64,7 +64,7 @@
     key_len = keys.shape[0]
     kv_heads = keys.shape[1] // HEAD_WIDTH
     group = width // HEAD_WIDTH // kv_heads
-    heads = min(4, group)
+    heads = min(8, group)
     steps = group // heads
     first = offset // block_rows
     grid_spec = pltpu.PrefetchScalarGridSpec(
@@ -214,15 +214,11 @@
     return bits
 
 
-def gather_row(value, size):
-    pieces, slots = value, [0]
-    halves = [pieces]
+def row_slots(size):
+    slots = [0]
     for bit in row_bits(size):
-        if len(halves) > 1:
-            pieces = jnp.concatenate(halves, axis=0)
-        halves = [pieces, swap(pieces, "row", bit, size)]
         slots = slots + [s ^ bit for s in slots]
-    return halves, slots
+    return slots
 
 
 def add_over_seq(value, size):
@@ -249,35 +245,6 @@
     me = lax.axis_index("col")
     last = size - 1
     return jnp.clip(last - t + me if way > 0 else t + me - last, 0, last)
-
-
-def chunk_list(length, block):
-    if length < 4 * block:
-        return [(at, block) for at in range(0, length, block)]
-    return [(0, block), (block, block)] + [(at, 2 * block) for at in range(2 * block, length, 2 * block)]
-
-
-def low_rank_steps(partial, col, n_col, n_row):
-    current = partial
-    for bit in row_bits(n_col):
-        half = current.shape[0] // 2
-        upper = jnp.bitwise_and(col, bit) != 0
-        keep = jnp.where(upper, current[half:], current[:half])
-        give = jnp.where(upper, current[:half], current[half:])
-        arrived = yield (lambda v, bit=bit: swap(v, "col", bit, n_col)), give.astype(BF16)
-        current = keep + arrived.astype(F32)
-    current = current.astype(BF16)
-    for bit in reversed(row_bits(n_col)):
-        arrived = yield (lambda v, bit=bit: swap(v, "col", bit, n_col)), current
-        upper = jnp.bitwise_and(col, bit) != 0
-        current = jnp.concatenate(
-            [jnp.where(upper, arrived, current), jnp.where(upper, current, arrived)]
-        )
-    current = current[None]
-    for bit in row_bits(n_row):
-        arrived = yield (lambda v, bit=bit: swap(v, "row", bit, n_row)), current
-        current = jnp.concatenate([current, arrived])
-    yield "done", current
 
 
 def tie(*values):
@@ -304,8 +271,7 @@
     seg_tiles = segment // TILE
     rank = frozen_down_factor.shape[1]
     block_rows = max(128, local_len // 4)
-    chunks = chunk_list(local_len, block_rows)
-    half_rows = n_row // 2
+    chunks = [(at, block_rows) for at in range(0, local_len, block_rows)]
     ways = (1, -1)
 
     here = jnp.stack([rotated_key_heads[0], value_head_states[0]])
@@ -325,129 +291,210 @@
         [starts[block_at] // key_block, (base + block_at + block_rows - 1) // key_block + 1, base[None]]
     ).astype(jnp.int32)
 
-    first_hop = {way: hop(cotangent, way, n_col, range(n_col)) for way in ways}
-
-    gathered, low_parts = [], []
-    for offset, rows in chunks:
-        part = attend_chunk(
-            queries[0], keys, values_t, bounds, starts[None], offset, rows, block_rows, key_block
-        )
-        low_parts.append(jnp.dot(part, frozen_down_factor, preferred_element_type=F32))
-        halves, slots = gather_row(part[None], n_row)
-        gathered.append(halves)
-    order = jnp.bitwise_xor(row, jnp.array(slots, jnp.int32))
+    whole_hop = {way: hop(cotangent, way, n_col, range(n_col)) for way in ways}
+    first_hop = [
+        {way: whole_hop[way][:, offset:offset + rows] for way in ways} for offset, rows in chunks
+    ]
 
     coords = tile_placement.reshape(-1, 2)
     coords, bounds = tie(coords, bounds)
     tile_in, tile_out = coords[:, 0], coords[:, 1]
     weight = add_tiles(output_projection_weight, correction_tiles.reshape(-1, TILE, TILE), tile_in, tile_out)
+    weight, bounds = tie(weight, bounds)
     tile_slot = jnp.mod(tile_out // seg_tiles - col, n_col)
     tile_out = tile_out % seg_tiles
 
+    slots = row_slots(n_row)
+    order = jnp.bitwise_xor(row, jnp.array(slots, jnp.int32))
     inverse = jnp.array([slots.index(s) for s in range(n_row)], jnp.int32)
     batch_slot = inverse[jnp.bitwise_xor(row, jnp.arange(n_row))]
 
-    jobs = []
-    for q, (offset, rows) in enumerate(chunks):
-        if rows == block_rows:
-            jobs.append((q, 0, n_row, jnp.concatenate(gathered[q])))
+    low_parts, gathered, terms = [], [], []
+    state = {"bounds": bounds}
+
+    def hold(*values):
+        state["bounds"] = tie(state["bounds"], *values)[0]
+
+    def attend(q):
+        offset, rows = chunks[q]
+        part = attend_chunk(
+            queries[0], keys, values_t, state["bounds"], starts[None], offset, rows, block_rows, key_block
+        )
+        part, state["bounds"] = tie(part, state["bounds"])
+        low_parts.append(jnp.dot(part, frozen_down_factor, preferred_element_type=F32))
+        return part
+
+    def gather(parts):
+        whole = jnp.stack(parts)[None]
+        for bit in row_bits(n_row):
+            moved = swap(whole, "row", bit, n_row)
+            state.setdefault("moved", []).append(moved)
+            whole = jnp.concatenate([whole, moved])
+        gathered.extend(whole[:, i] for i in range(len(parts)))
+
+    late_parts = []
+    for q in range(len(chunks)):
+        if q == 3:
+            hold(state["moved"][0])
+        part = attend(q)
+        if q < 2:
+            gather([part])
         else:
-            jobs.extend((q, h * half_rows, half_rows, gathered[q][h]) for h in range(2))
-    jobs = [
-        (q, lead, count, jnp.dot(part.reshape(count * chunks[q][1], width), weight, preferred_element_type=F32))
-        for q, lead, count, part in jobs
-    ]
-
-    low_steps = low_rank_steps(jnp.concatenate(low_parts), col, n_col, n_row)
-    low_next = next(low_steps)
-    low_pending, low_done = None, None
-    last = [{}, {}]
-    got = [None] * len(jobs)
-    streams = []
-    for q, lead, count, _ in jobs:
+            late_parts.append(part)
+    if late_parts:
+        gather(late_parts)
+
+    def project(q):
+        terms.append(
+            jnp.dot(gathered[q].reshape(n_row * chunks[q][1], width), weight, preferred_element_type=F32)
+        )
+
+    got = [None] * len(chunks)
+    streams = [{way: [first_hop[q][way]] for way in ways} for q in range(len(chunks))]
+
+    def launch(q, t, before):
+        sends = []
+        for way in ways:
+            send = lax.dynamic_slice_in_dim(terms[q], target(way, t, n_col) * segment, segment, 1)
+            if t > 0:
+                send = send + got[q][way].astype(F32)
+            send = send.astype(BF16)
+            if t + 1 < n_col - 1:
+                place = col if way > 0 else n_col - 1 - col
+                send = jnp.where(place <= t, send, streams[q][way][-1].reshape(send.shape))
+            sends.append(send)
+        tied = tie(*sends, *before)
+        got[q] = {way: hop(tied[i], way, n_col, range(n_col)) for i, way in enumerate(ways)}
+        if t + 1 < n_col - 1:
+            for way in ways:
+                streams[q][way].append(got[q][way].reshape(n_row, chunks[q][1], segment))
+        return tied[len(ways):]
+
+    def cot_of(q):
         offset, rows = chunks[q]
-        streams.append({way: [first_hop[way][lead:lead + count, offset:offset + rows]] for way in ways})
-    for first in range(0, len(jobs), 2):
+        parts = [cotangent[:, offset:offset + rows]] + by_slot(streams[q][1], streams[q][-1], n_col)
+        return jnp.concatenate([part[None] for part in parts])
+
+    def add_up(q, cot, total):
+        offset, rows = chunks[q]
+        return up_grad(
+            col,
+            state["low_ordered"][:, offset:offset + rows].reshape(n_row * rows, rank),
+            cot.reshape(n_col, n_row * rows, segment),
+            total,
+        )
+
+    cots = {}
+    early = len(chunks) // 2
+
+    def side():
+        current = jnp.concatenate(low_parts)
+        for bit in row_bits(n_col):
+            half = current.shape[0] // 2
+            upper = jnp.bitwise_and(col, bit) != 0
+            keep = jnp.where(upper, current[half:], current[:half])
+            give = jnp.where(upper, current[:half], current[half:])
+            arrived = yield (lambda v, bit=bit: swap(v, "col", bit, n_col)), give.astype(BF16), 3
+            current = keep + arrived.astype(F32)
+        current = current.astype(BF16)
+        for bit in reversed(row_bits(n_col)):
+            arrived = yield (lambda v, bit=bit: swap(v, "col", bit, n_col)), current, 2
+            upper = jnp.bitwise_and(col, bit) != 0
+            current = jnp.concatenate(
+                [jnp.where(upper, arrived, current), jnp.where(upper, current, arrived)]
+            )
+        current = current[None]
+        for bit in row_bits(n_row):
+            arrived = yield (lambda v, bit=bit: swap(v, "row", bit, n_row)), current, 1
+            current = jnp.concatenate([current, arrived])
+        state["low"] = current
+        state["low_ordered"] = current[batch_slot]
+        while any(q not in cots for q in range(early)):
+            yield None
+        total = jnp.zeros((rank, out_width), F32)
+        for q in range(early):
+            total = add_up(q, cots[q], total)
+        if n_seq == 2:
+            total = lax.reduce_precision(total, exponent_bits=8, mantissa_bits=7)
+            arrived = yield (lambda v: swap(v, "seq", 1, n_seq)), total.astype(BF16), 99
+            state["up_early"] = total + arrived.astype(F32)
+        else:
+            state["up_early"] = lax.psum(total, "seq")
+
+    lanes = [list(range(lane, len(chunks), 2)) for lane in range(2)]
+    rounds = []
+    for at in range(len(lanes[0])):
         for t in range(n_col - 1):
-            for lane, at in enumerate(range(first, min(first + 2, len(jobs)))):
-                q, lead, count, terms = jobs[at]
-                sends = {}
-                for way in ways:
-                    send = lax.dynamic_slice_in_dim(terms, target(way, t, n_col) * segment, segment, 1)
-                    if t > 0:
-                        send = send + got[at][way].astype(F32)
-                    send = send.astype(BF16)
-                    if t + 1 < n_col - 1:
-                        place = col if way > 0 else n_col - 1 - col
-                        send = jnp.where(place <= t, send, streams[at][way][-1].reshape(send.shape))
-                    sends[way] = send
-                before = [last[lane][way] for way in ways] if last[lane] else []
-                if low_pending is not None and lane == 1:
-                    before = before + [low_pending]
-                tied = tie(*[sends[way] for way in ways], *before)
-                if low_pending is not None and lane == 1:
-                    low_next = low_steps.send(tied[-1])
-                    low_pending = None
-                    if low_next[0] == "done":
-                        low_done = low_next[1]
-                        low_next = None
-                arrived = {way: hop(tied[i], way, n_col, range(n_col)) for i, way in enumerate(ways)}
-                if lane == 0 and low_next is not None and low_pending is None:
-                    move, value = low_next
-                    if before:
-                        value, *_ = tie(value, *tied[len(ways):])
-                    low_pending = move(value)
-                last[lane] = arrived
-                got[at] = arrived
-                if t + 1 < n_col - 1:
-                    for way in ways:
-                        streams[at][way].append(
-                            arrived[way].reshape(count, chunks[q][1], segment)
-                        )
-    while low_done is None:
-        if low_pending is None:
-            low_pending = low_next[0](low_next[1])
-        low_next = low_steps.send(low_pending)
-        low_pending = None
-        if low_next[0] == "done":
-            low_done = low_next[1]
-    low = low_done
-    low_ordered = low[batch_slot]
+            for lane in range(2):
+                if at < len(lanes[lane]):
+                    rounds.append((lane, lanes[lane][at], t))
+    last = [None, None]
+    steps = side()
+    pending, wait, over = None, 0, False
+    tile_sum = jnp.zeros((coords.shape[0], TILE, TILE), F32)
+    tile_due = []
+
+    def advance(value):
+        try:
+            item = steps.send(value)
+        except StopIteration:
+            return None, 0, True
+        if item is None:
+            return None, 0, False
+        return item[0](item[1]), item[2], False
+
+    pending, _, over = advance(None)
+    for at, (lane, q, t) in enumerate(rounds):
+        if q == len(terms):
+            project(q)
+        before = [last[lane][way] for way in ways] if last[lane] else []
+        if at == 5 and len(terms) < len(chunks):
+            project(len(terms))
+            before.append(terms[-1])
+        take_side = pending is not None and wait <= 0
+        if take_side:
+            before.append(pending)
+        if tile_due and tile_due[0][0] <= at:
+            before.insert(0, tile_due.pop(0)[1])
+        seen = list(launch(q, t, before))
+        for c in range(len(chunks)):
+            if c not in cots and all(len(streams[c][way]) == n_col - 1 for way in ways):
+                cots[c] = cot_of(c)
+                tile_sum = tile_sum + tile_grads([gathered[c]], cots[c], tile_in, tile_slot, tile_out, order)
+                if at + 3 < len(rounds):
+                    tile_due.append((at + 3, tile_sum))
+        wait -= 1
+        if take_side:
+            pending, wait, over = advance(seen.pop())
+            wait -= 1
+        elif pending is None and not over:
+            pending, wait, over = advance(None)
+            wait -= 1
+        last[lane] = got[q]
+    while not over:
+        pending, _, over = advance(pending)
+    low = state["low"]
 
     up_here = lax.dynamic_slice_in_dim(trained_up_factor, col * segment, segment, 1)
     projected = jnp.zeros((n_row, local_len, segment), BF16)
-    for at, (q, lead, count, terms) in enumerate(jobs):
-        offset, rows = chunks[q]
-        for j in range(count):
-            low_term = jnp.dot(low[lead + j, offset:offset + rows], up_here, preferred_element_type=F32)
-            mine = lax.dynamic_slice(terms, (j * rows, col * segment), (rows, segment))
+    for q, (offset, rows) in enumerate(chunks):
+        for j in range(n_row):
+            low_term = jnp.dot(low[j, offset:offset + rows], up_here, preferred_element_type=F32)
+            mine = lax.dynamic_slice(terms[q], (j * rows, col * segment), (rows, segment))
             sums = mine + LOW_RANK_FACTOR * low_term
             for way in ways:
-                sums = sums + got[at][way][j * rows:(j + 1) * rows].astype(F32)
-            projected = lax.dynamic_update_slice(
-                projected, sums.astype(BF16)[None], (order[lead + j], offset, 0)
-            )
-
-    tile_sum = jnp.zeros((coords.shape[0], TILE, TILE), F32)
-    up_total = jnp.zeros((rank, out_width), F32)
-    for q, (offset, rows) in enumerate(chunks):
-        parts = []
-        for at, job in enumerate(jobs):
-            if job[0] == q:
-                own = cotangent[job[1]:job[1] + job[2], offset:offset + rows]
-                parts.append([own] + by_slot(streams[at][1], streams[at][-1], n_col))
-        cot = jnp.concatenate(
-            [jnp.concatenate([part[k] for part in parts])[None] for k in range(n_col)]
-        )
-        tile_sum = tile_sum + tile_grads(gathered[q], cot, tile_in, tile_slot, tile_out, order)
-        up_total = up_grad(
-            col,
-            low_ordered[:, offset:offset + rows].reshape(n_row * rows, rank),
-            cot.reshape(n_col, n_row * rows, segment),
-            up_total,
-        )
-
-    up_gradient = add_over_seq(up_total, n_seq)
+                sums = sums + got[q][way][j * rows:(j + 1) * rows].astype(F32)
+            projected = lax.dynamic_update_slice(projected, sums.astype(BF16)[None], (order[j], offset, 0))
+
+    total = jnp.zeros((rank, out_width), F32)
+    for q in range(early, len(chunks)):
+        total = add_up(q, cots[q], total)
+    if n_seq == 2:
+        total = lax.reduce_precision(total, exponent_bits=8, mantissa_bits=7)
+        total = total + swap(total.astype(BF16), "seq", 1, n_seq).astype(F32)
+    else:
+        total = lax.psum(total, "seq")
+    up_gradient = state["up_early"] + total
     tile_total = add_over_seq(tile_sum, n_seq)
     return projected, up_gradient, tile_total.reshape(correction_tiles.shape)
 

time: 589 us -> 512 us (0.87); the launches traced: 579 us -> 511 us
  waiting for transfers between devices: 167 us -> 84.6 us
  Pallas kernels: 78.9 us -> 93.8 us
  starting transfers between devices: 130 us -> 116 us
  other arithmetic: 80.7 us -> 87.5 us
  local copies, waits for them, and re-layouts: 36.6 us -> 42.7 us
    ppermute x26, waiting for transfers between devices: 117 us -> 61.9 us  [hop(): return lax.ppermute(value, 'col', pairs)]
    ppermute x15 -> x16, waiting for transfers between devices: 49.3 us -> 22.7 us  [swap(): return lax.ppermute(value, axis, [(i, i ^ bit) for i in range(size)])]
    ppermute x15 -> x16, starting transfers between devices: 55.6 us -> 34.4 us  [swap(): return lax.ppermute(value, axis, [(i, i ^ bit) for i in range(size)])]
    pallas_call x3 -> x4, Pallas kernels: 46.7 us -> 59.8 us  [attend_chunk(): pl.pallas_call(functools.partial(attend_kernel, heads=heads, key_block=ke...]
    squeeze x0 -> x2, other arithmetic: none -> 9.12 us  [gather(): gathered.extend((whole[:, i] for i in range(len(parts))))]
    ppermute x26, starting transfers between devices: 74.8 us -> 82 us  [hop(): return lax.ppermute(value, 'col', pairs)]
    squeeze x0 -> x1, local copies, waits for them, and re-layouts: none -> 6.38 us  [gather(): gathered.extend((whole[:, i] for i in range(len(parts))))]
    broadcast_in_dim x3 -> x0, local copies, waits for them, and re-layouts: 6.26 us -> none  [the longest x2 6.03 us: local(): jnp.concatenate([part[k] for part in parts])[None]]
  transfers between devices with their start and end apart: 41 -> 42, of which waited for: 17 -> 12; matrix products, arithmetic and copies ran while one was open for 31% -> 37% of each run, Pallas kernels for 14% -> 18%
where the time goes in v2:
time: 512 us; the launch traced here: 511 us
  starting transfers between devices  116 us (23%)
  Pallas kernels  93.8 us (18%)
  other arithmetic  87.5 us (17%)
  waiting for transfers between devices  84.6 us (17%)
  matrix products  75.7 us (15%)
  local copies, waits for them, and re-layouts  42.7 us (8%)
  between operations  9.88 us (2%)
    ppermute x26, starting transfers between devices, hop(): return lax.ppermute(value, 'col', pairs)  82 us
    ppermute x26, waiting for transfers between devices, hop(): return lax.ppermute(value, 'col', pairs)  61.9 us
    pallas_call x4, Pallas kernels, attend_chunk(): pl.pallas_call(functools.partial(attend_kernel, heads=heads, key_block=ke...  59.8 us
    dot_general x4, matrix products, project(): jnp.dot(gathered[q].reshape(n_row * chunks[q][1], width), weight, preferr...  45.9 us
    ppermute x16, starting transfers between devices, swap(): return lax.ppermute(value, axis, [(i, i ^ bit) for i in range(size)])  34.4 us
    dot_general x16, matrix products, local(): jnp.dot(low[j, offset:offset + rows], up_here, preferred_element_type=F32)  28 us
    select_n x8, other arithmetic, launch(): send = jnp.where(place <= t, send, streams[q][way][-1].reshape(send.shape))  23.5 us
    ppermute x16, waiting for transfers between devices, swap(): return lax.ppermute(value, axis, [(i, i ^ bit) for i in range(size)])  22.7 us
  transfers between devices with their start and end apart: 42, of which 12 were waited for; matrix products, arithmetic and copies ran while one was open for 37% of the time, Pallas kernels for 18%

profile of v2, /device:TPU:0, one launch (start us, length us, event | category | flops | bytes accessed | tf_op | source)
XLA Modules:
  0.0 510.7 jit_solution(15873585948697461449)
XLA Ops:
  2.1 7.7 %collective-permute-start.5 = (bf16[4,1024,512]{2,1,0:T(8,128)(2,1)}, bf16[4,1024,512]{2,1,0:T(8,128)(2,1)}, u32[]{:S(2)}, u32[]{:S(2)}) collective-permute-start(bf16[4,1024,512]{2,1,0:T(8,128)(2,1)} %param.21), channel_id=1, source_target_pairs={{0,2},{2,4},{4,6},{1,3},{3,5},{5,7},{8,10},{10,12},{12,14},{9,11},... | collective-permute-start | bytes 12582920 | tf_op jit(solution)/shard_map/ppermute | solution.py:234
  18.3 13.2 %add_tiles.1 = bf16[2048,2048]{1,0:T(8,128)(2,1)} custom-call(s32[5]{0:T(128)} %get-tuple-element.164.in_ref, s32[5]{0:T(128)} %get-tuple-element.163.out_tile_ref, bf16[2048,2048]{1,0:T(8,128)(2,1)} %w_ref.1, bf16[5,128,128]{2,1,0:T(8,128)(2,1)} %bitcast.311), custom_call_target="tpu_custom_call" | custom-call | bytes 16777216 | tf_op jit(solution)/shard_map/add_tiles/pallas_call | solution.py:117
  32.1 6.0 %collective-permute-done = bf16[2,1024,256]{1,2,0:T(8,128)(2,1)S(1)} collective-permute-done((bf16[2,1024,256]{1,2,0:T(8,128)(2,1)}, bf16[2,1024,256]{1,2,0:T(8,128)(2,1)S(1)}, u32[]{:S(2)}, u32[]{:S(2)}) %collective-permute-start) | collective-permute-done | bytes 1048608 | tf_op jit(solution)/shard_map/ppermute | solution.py:205
  43.3 7.1 %attention.4 = bf16[256,2048]{1,0:T(8,128)(2,1)S(1)} custom-call(s32[9]{0:T(128)S(1)} %pad_add_fusion.bounds_ref, bf16[1024,2048]{1,0:T(8,128)(2,1)S(1)} %bitcast.264, bf16[2048,256]{1,0:T(8,128)(2,1)S(1)} %copy.33.k_ref, bf16[256,2048]{1,0:T(8,128)(2,1)S(1)} %copy-done.7, s32[1,1024]{1,0:T(1,128)S(1)} %bitcast.248), custom_call_target="tpu_custom_call" | custom-call | flops 2863300608 | bytes 2097152 | tf_op jit(solution)/shard_map/attention/pallas_call | solution.py:82
  55.7 12.3 %attention.5 = bf16[256,2048]{1,0:T(8,128)(2,1)S(1)} custom-call(s32[9]{0:T(128)S(1)} %pad_add_fusion.bounds_ref, bf16[1024,2048]{1,0:T(8,128)(2,1)S(1)} %bitcast.265, bf16[2048,256]{1,0:T(8,128)(2,1)S(1)} %copy.33.k_ref, bf16[256,2048]{1,0:T(8,128)(2,1)S(1)} %copy-done.8, s32[1,1024]{1,0:T(1,128)S(1)} %bitcast.249), custom_call_target="tpu_custom_call" | custom-call | flops 2863300608 | bytes 2097152 | tf_op jit(solution)/shard_map/attention/pallas_call | solution.py:82
  68.5 6.0 %collective-permute-done.1 = bf16[1,1,256,2048]{3,2,0,1:T(8,128)(2,1)} collective-permute-done((bf16[1,1,256,2048]{3,2,0,1:T(8,128)(2,1)S(1)}, bf16[1,1,256,2048]{3,2,0,1:T(8,128)(2,1)}, u32[]{:S(2)}, u32[]{:S(2)}) %collective-permute-start.1) | collective-permute-done | bytes 1048608 | tf_op jit(solution)/shard_map/ppermute | solution.py:205
  77.9 17.5 %attention.6 = bf16[256,2048]{1,0:T(8,128)(2,1)S(1)} custom-call(s32[9]{0:T(128)S(1)} %pad_add_fusion.bounds_ref, bf16[1024,2048]{1,0:T(8,128)(2,1)S(1)} %bitcast.266, bf16[2048,256]{1,0:T(8,128)(2,1)S(1)} %copy.33.k_ref, bf16[256,2048]{1,0:T(8,128)(2,1)S(1)} %copy-done.8, s32[1,1024]{1,0:T(1,128)S(1)} %bitcast.250), custom_call_target="tpu_custom_call" | custom-call | flops 2863300608 | bytes 2097152 | tf_op jit(solution)/shard_map/attention/pallas_call | solution.py:82
  95.8 22.9 %attention.7 = bf16[256,2048]{1,0:T(8,128)(2,1)S(1)} custom-call(s32[9]{0:T(128)S(1)} %pad_add_fusion.bounds_ref, bf16[1024,2048]{1,0:T(8,128)(2,1)S(1)} %bitcast.267, bf16[2048,256]{1,0:T(8,128)(2,1)S(1)} %copy.33.k_ref, bf16[256,2048]{1,0:T(8,128)(2,1)S(1)} %copy-done.8, s32[1,1024]{1,0:T(1,128)S(1)} %bitcast.251), custom_call_target="tpu_custom_call" | custom-call | flops 2863300608 | bytes 2097152 | tf_op jit(solution)/shard_map/attention/pallas_call | solution.py:82
  130.5 8.9 %fusion.88 = f32[1024,2048]{1,0:T(8,128)S(1)} fusion(bf16[1024,2048]{1,0:T(8,128)(2,1)S(1)} %bitcast.302, bf16[2048,2048]{1,0:T(8,128)(2,1)S(1)} %bitcast.301), kind=kOutput, calls=%fused_computation.236 | convolution fusion | flops 8589934592 | bytes 20971520 | tf_op jit(solution)/shard_map/dot_general | solution.py:349
  146.4 5.3 %fusion.80 = (bf16[4,256,2048]{2,1,0:T(8,128)(2,1)}, bf16[4,1,256,2048]{3,2,0,1:T(8,128)(2,1)}) fusion(bf16[2,1,256,2048]{3,2,0,1:T(8,128)(2,1)} %collective-permute-done.8, bf16[1,1,256,2048]{3,2,0,1:T(8,128)(2,1)S(1)} %collective-permute-done.7, bf16[1,1,256,2048]{3,2,0,1:T(8,128)(2,1)S(1)} %bitcast.257), kind=kLoop, calls=%fused_computation.228 | loop fusion | flops 4194304 | bytes 12582912 | tf_op jit(solution)/shard_map/squeeze | solution.py:333
  151.7 10.8 %fusion.90 = f32[1024,2048]{1,0:T(8,128)S(1)} fusion(bf16[1024,2048]{1,0:T(8,128)(2,1)} %bitcast.303, bf16[2048,2048]{1,0:T(8,128)(2,1)S(1)} %bitcast.301), kind=kOutput, calls=%fused_computation.238 | convolution fusion | flops 8589934592 | bytes 20971520 | tf_op jit(solution)/shard_map/dot_general | solution.py:349
  165.1 5.2 %collective-permute-start.9 = (bf16[1024,512]{1,0:T(8,128)(2,1)S(1)}, bf16[1024,512]{1,0:T(8,128)(2,1)S(1)}, u32[]{:S(2)}, u32[]{:S(2)}) collective-permute-start(bf16[1024,512]{1,0:T(8,128)(2,1)S(1)} %get-tuple-element.57), channel_id=1, source_target_pairs={{0,2},{2,4},{4,6},{1,3},{3,5},{5,7},{8,10},{10,12},{12,14},{9,11},... | collective-permute-start | bytes 3145736 | tf_op jit(solution)/shard_map/ppermute | solution.py:234
  177.5 4.9 fusion.3
  183.7 12.0 %collective-permute-done.10 = bf16[1024,512]{1,0:T(8,128)(2,1)S(1)} collective-permute-done((bf16[1024,512]{1,0:T(8,128)(2,1)S(1)}, bf16[1024,512]{1,0:T(8,128)(2,1)S(1)}, u32[]{:S(2)}, u32[]{:S(2)}) %collective-permute-start.10) | collective-permute-done | bytes 1048608 | tf_op jit(solution)/shard_map/ppermute | solution.py:234
  210.6 5.7 %fusion.83 = (bf16[4,256,512]{2,1,0:T(8,128)(2,1)}, bf16[1,4,256,512]{3,2,1,0:T(8,128)(2,1)S(1)}, bf16[1,4,256,512]{3,2,1,0:T(8,128)(2,1)S(1)}, bf16[1,4,256,512...) fusion(bf16[4,1024,512]{2,1,0:T(8,128)(2,1)} %param.21), kind=kLoop, calls=%fused_computation.231 | loop fusion | bytes 12582912 | tf_op jit(solution)/shard_map/slice | solution.py:375
  216.2 4.7 collective-permute-start.13
  225.0 4.8 collective-permute-start.23
  229.8 13.7 %collective-permute-done.14 = bf16[1024,512]{1,0:T(8,128)(2,1)} collective-permute-done((bf16[1024,512]{1,0:T(8,128)(2,1)}, bf16[1024,512]{1,0:T(8,128)(2,1)}, u32[]{:S(2)}, u32[]{:S(2)}) %collective-permute-start.14) | collective-permute-done | bytes 1048608 | tf_op jit(solution)/shard_map/ppermute | solution.py:234
  270.9 6.4 %slice_bitcast_fusion.14 = (bf16[4,256,2048]{2,1,0:T(8,128)(2,1)}, bf16[4,256,2048]{2,1,0:T(8,128)(2,1)}, bf16[4,1,256,2048]{3,2,0,1:T(8,128)(2,1)}, bf16[4,1,256,2048]{3,2,0,1:T(8,128)(2,1)}) fusion(bf16[4,2,256,2048]{3,2,0,1:T(8,128)(2,1)S(1)} %pad_maximum_fusion), kind=kLoop, calls=%fused_computation.226 | loop fusion | bytes 25165824 | tf_op jit(solution)/shard_map/squeeze | solution.py:333
  277.3 12.6 %fusion.95 = f32[1024,2048]{1,0:T(8,128)S(1)} fusion(bf16[1024,2048]{1,0:T(8,128)(2,1)} %bitcast.305, bf16[2048,2048]{1,0:T(8,128)(2,1)} %add_tiles.1), kind=kOutput, calls=%fused_computation.243 | convolution fusion | flops 8589934592 | bytes 20971520 | tf_op jit(solution)/shard_map/dot_general | solution.py:349
  292.3 5.2 %collective-permute-start.25 = (bf16[1024,512]{1,0:T(8,128)(2,1)}, bf16[1024,512]{1,0:T(8,128)(2,1)}, u32[]{:S(2)}, u32[]{:S(2)}) collective-permute-start(bf16[1024,512]{1,0:T(8,128)(2,1)} %get-tuple-element.73), channel_id=1, source_target_pairs={{0,2},{2,4},{4,6},{1,3},{3,5},{5,7},{8,10},{10,12},{12,14},{9,11},... | collective-permute-start | bytes 3145736 | tf_op jit(solution)/shard_map/ppermute | solution.py:234
  301.7 5.4 %collective-permute-start.20 = (bf16[1024,512]{1,0:T(8,128)(2,1)}, bf16[1024,512]{1,0:T(8,128)(2,1)}, u32[]{:S(2)}, u32[]{:S(2)}) collective-permute-start(bf16[1024,512]{1,0:T(8,128)(2,1)} %get-tuple-element.67), channel_id=1, source_target_pairs={{0,2},{2,4},{4,6},{1,3},{3,5},{5,7},{8,10},{10,12},{12,14},{9,11},... | collective-permute-start | bytes 3145736 | tf_op jit(solution)/shard_map/ppermute | solution.py:234
  308.5 13.7 %fusion.89 = f32[1024,2048]{1,0:T(8,128)} fusion(bf16[1024,2048]{1,0:T(8,128)(2,1)S(1)} %bitcast.304, bf16[2048,2048]{1,0:T(8,128)(2,1)} %add_tiles.1), kind=kOutput, calls=%fused_computation.237 | convolution fusion | flops 8589934592 | bytes 20971520 | tf_op jit(solution)/shard_map/dot_general | solution.py:349
  325.2 10.5 %collective-permute-done.22 = bf16[512,256]{1,0:T(8,128)(2,1)} collective-permute-done((bf16[512,256]{1,0:T(8,128)(2,1)S(1)}, bf16[512,256]{1,0:T(8,128)(2,1)}, u32[]{:S(2)}, u32[]{:S(2)}) %collective-permute-start.22) | collective-permute-done | bytes 262176 | tf_op jit(solution)/shard_map/ppermute | solution.py:205
  335.7 10.4 %collective-permute-done.20 = bf16[1024,512]{1,0:T(8,128)(2,1)} collective-permute-done((bf16[1024,512]{1,0:T(8,128)(2,1)}, bf16[1024,512]{1,0:T(8,128)(2,1)}, u32[]{:S(2)}, u32[]{:S(2)}) %collective-permute-start.20) | collective-permute-done | bytes 1048608 | tf_op jit(solution)/shard_map/ppermute | solution.py:234
  346.1 5.1 collective-permute-done.21
  355.2 7.2 %collective-permute-start.28 = (bf16[1024,512]{1,0:T(8,128)(2,1)S(1)}, bf16[1024,512]{1,0:T(8,128)(2,1)S(1)}, u32[]{:S(2)}, u32[]{:S(2)}) collective-permute-start(bf16[1024,512]{1,0:T(8,128)(2,1)S(1)} %get-tuple-element.76), channel_id=1, source_target_pairs={{0,2},{2,4},{4,6},{1,3},{3,5},{5,7},{8,10},{10,12},{12,14},{9,11},... | collective-permute-start | bytes 3145736 | tf_op jit(solution)/shard_map/ppermute | solution.py:234
  363.7 4.8 fusion.5
  373.6 5.6 %collective-permute-start.31 = (bf16[1024,512]{1,0:T(8,128)(2,1)}, bf16[1024,512]{1,0:T(8,128)(2,1)}, u32[]{:S(2)}, u32[]{:S(2)}) collective-permute-start(bf16[1024,512]{1,0:T(8,128)(2,1)} %get-tuple-element.79), channel_id=1, source_target_pairs={{0,2},{2,4},{4,6},{1,3},{3,5},{5,7},{8,10},{10,12},{12,14},{9,11},... | collective-permute-start | bytes 3145736 | tf_op jit(solution)/shard_map/ppermute | solution.py:234
  408.5 19.9 %collective-permute-start.39 = (bf16[256,2048]{1,0:T(8,128)(2,1)S(1)}, bf16[256,2048]{1,0:T(8,128)(2,1)S(1)}, u32[]{:S(2)}, u32[]{:S(2)}) collective-permute-start(bf16[256,2048]{1,0:T(8,128)(2,1)S(1)} %reduce-precision_convert_fusion.1), channel_id=1, source_target_pairs={{0,1},{1,0},{2,3},{3,2},{4,5},{5,4},{6,7},{7,6},{8,9},{9,8},{10,11... | collective-permute-start | bytes 3145736 | tf_op jit(solution)/shard_map/ppermute | solution.py:205
  430.8 4.7 collective-permute-start.33
  490.0 10.2 %collective-permute-done.37 = bf16[1024,512]{1,0:T(8,128)(2,1)S(1)} collective-permute-done((bf16[1024,512]{1,0:T(8,128)(2,1)S(1)}, bf16[1024,512]{1,0:T(8,128)(2,1)S(1)}, u32[]{:S(2)}, u32[]{:S(2)}) %collective-permute-start.37) | collective-permute-done | bytes 1048608 | tf_op jit(solution)/shard_map/ppermute | solution.py:234
  (293 shorter events, 210.5 us)
Async XLA Ops:
  0.7 121.6 %collective-permute-start.6 = (bf16[4,1024,512]{2,1,0:T(8,128)(2,1)}, bf16[4,1024,512]{2,1,0:T(8,128)(2,1)}, u32[]{:S(2)}, u32[]{:S(2)}) collective-permute-start(bf16[4,1024,512]{2,1,0:T(8,128)(2,1)} %param.21), channel_id=1, source_target_pairs={{6,4},{4,2},{2,0},{7,5},{5,3},{3,1},{14,12},{12,10},{10,8},{15,13}... | collective-permute-start | bytes 12582920 | tf_op jit(solution)/shard_map/ppermute | solution.py:234
  2.1 126.6 %collective-permute-start.5 = (bf16[4,1024,512]{2,1,0:T(8,128)(2,1)}, bf16[4,1024,512]{2,1,0:T(8,128)(2,1)}, u32[]{:S(2)}, u32[]{:S(2)}) collective-permute-start(bf16[4,1024,512]{2,1,0:T(8,128)(2,1)} %param.21), channel_id=1, source_target_pairs={{0,2},{2,4},{4,6},{1,3},{3,5},{5,7},{8,10},{10,12},{12,14},{9,11},... | collective-permute-start | bytes 12582920 | tf_op jit(solution)/shard_map/ppermute | solution.py:234
  75.9 48.9 %collective-permute-start.2 = (bf16[2,1,256,2048]{3,2,0,1:T(8,128)(2,1)S(1)}, bf16[2,1,256,2048]{3,2,0,1:T(8,128)(2,1)}, u32[]{:S(2)}, u32[]{:S(2)}) collective-permute-start(bf16[2,1,256,2048]{3,2,0,1:T(8,128)(2,1)S(1)} %pad_maximum_fusion.12), channel_id=1, source_target_pairs={{0,8},{8,0},{16,24},{24,16},{1,9},{9,1},{17,25},{25,17},{2,10},{10... | collective-permute-start | bytes 6291464 | tf_op jit(solution)/shard_map/ppermute | solution.py:205
  76.4 45.4 %collective-permute-start.7 = (bf16[1,1,256,2048]{3,2,0,1:T(8,128)(2,1)S(1)}, bf16[1,1,256,2048]{3,2,0,1:T(8,128)(2,1)S(1)}, u32[]{:S(2)}, u32[]{:S(2)}) collective-permute-start(bf16[1,1,256,2048]{3,2,0,1:T(8,128)(2,1)S(1)} %bitcast.255), channel_id=1, source_target_pairs={{0,16},{8,24},{16,0},{24,8},{1,17},{9,25},{17,1},{25,9},{2,18},{10... | collective-permute-start | bytes 3145736 | tf_op jit(solution)/shard_map/ppermute | solution.py:205
  122.3 48.2 %collective-permute-start.3 = (bf16[1,2,256,2048]{3,2,0,1:T(8,128)(2,1)S(1)}, bf16[1,2,256,2048]{3,2,0,1:T(8,128)(2,1)}, u32[]{:S(2)}, u32[]{:S(2)}) collective-permute-start(bf16[1,2,256,2048]{3,2,0,1:T(8,128)(2,1)S(1)} %maximum_bitcast_fusion), channel_id=1, source_target_pairs={{0,16},{8,24},{16,0},{24,8},{1,17},{9,25},{17,1},{25,9},{2,18},{10... | collective-permute-start | bytes 6291464 | tf_op jit(solution)/shard_map/ppermute | solution.py:205
  142.2 33.3 %collective-permute-start.15 = (bf16[1024,512]{1,0:T(8,128)(2,1)}, bf16[1024,512]{1,0:T(8,128)(2,1)}, u32[]{:S(2)}, u32[]{:S(2)}) collective-permute-start(bf16[1024,512]{1,0:T(8,128)(2,1)} %get-tuple-element.62), channel_id=1, source_target_pairs={{0,2},{2,4},{4,6},{1,3},{3,5},{5,7},{8,10},{10,12},{12,14},{9,11},... | collective-permute-start | bytes 3145736 | tf_op jit(solution)/shard_map/ppermute | solution.py:234
  145.1 32.4 %collective-permute-start.16 = (bf16[1024,512]{1,0:T(8,128)(2,1)}, bf16[1024,512]{1,0:T(8,128)(2,1)}, u32[]{:S(2)}, u32[]{:S(2)}) collective-permute-start(bf16[1024,512]{1,0:T(8,128)(2,1)} %get-tuple-element.63), channel_id=1, source_target_pairs={{6,4},{4,2},{2,0},{7,5},{5,3},{3,1},{14,12},{12,10},{10,8},{15,13}... | collective-permute-start | bytes 3145736 | tf_op jit(solution)/shard_map/ppermute | solution.py:234
  163.5 32.1 %collective-permute-start.10 = (bf16[1024,512]{1,0:T(8,128)(2,1)S(1)}, bf16[1024,512]{1,0:T(8,128)(2,1)S(1)}, u32[]{:S(2)}, u32[]{:S(2)}) collective-permute-start(bf16[1024,512]{1,0:T(8,128)(2,1)S(1)} %get-tuple-element.58), channel_id=1, source_target_pairs={{6,4},{4,2},{2,0},{7,5},{5,3},{3,1},{14,12},{12,10},{10,8},{15,13}... | collective-permute-start | bytes 3145736 | tf_op jit(solution)/shard_map/ppermute | solution.py:234
  165.1 33.7 %collective-permute-start.9 = (bf16[1024,512]{1,0:T(8,128)(2,1)S(1)}, bf16[1024,512]{1,0:T(8,128)(2,1)S(1)}, u32[]{:S(2)}, u32[]{:S(2)}) collective-permute-start(bf16[1024,512]{1,0:T(8,128)(2,1)S(1)} %get-tuple-element.57), channel_id=1, source_target_pairs={{0,2},{2,4},{4,6},{1,3},{3,5},{5,7},{8,10},{10,12},{12,14},{9,11},... | collective-permute-start | bytes 3145736 | tf_op jit(solution)/shard_map/ppermute | solution.py:234
  174.4 92.7 %collective-permute-start.4 = (bf16[2,2,256,2048]{3,2,0,1:T(8,128)(2,1)}, bf16[2,2,256,2048]{3,2,0,1:T(8,128)(2,1)}, u32[]{:S(2)}, u32[]{:S(2)}) collective-permute-start(bf16[2,2,256,2048]{3,2,0,1:T(8,128)(2,1)} %pad_maximum_fusion.2), channel_id=1, source_target_pairs={{0,8},{8,0},{16,24},{24,16},{1,9},{9,1},{17,25},{25,17},{2,10},{10... | collective-permute-start | bytes 12582920 | tf_op jit(solution)/shard_map/ppermute | solution.py:205
  182.4 38.7 %collective-permute-start.18 = (bf16[1024,512]{1,0:T(8,128)(2,1)}, bf16[1024,512]{1,0:T(8,128)(2,1)}, u32[]{:S(2)}, u32[]{:S(2)}) collective-permute-start(bf16[1024,512]{1,0:T(8,128)(2,1)} %get-tuple-element.65), channel_id=1, source_target_pairs={{6,4},{4,2},{2,0},{7,5},{5,3},{3,1},{14,12},{12,10},{10,8},{15,13}... | collective-permute-start | bytes 3145736 | tf_op jit(solution)/shard_map/ppermute | solution.py:234
  195.6 25.5 %collective-permute-start.17 = (bf16[1024,512]{1,0:T(8,128)(2,1)}, bf16[1024,512]{1,0:T(8,128)(2,1)}, u32[]{:S(2)}, u32[]{:S(2)}) collective-permute-start(bf16[1024,512]{1,0:T(8,128)(2,1)} %get-tuple-element.64), channel_id=1, source_target_pairs={{0,2},{2,4},{4,6},{1,3},{3,5},{5,7},{8,10},{10,12},{12,14},{9,11},... | collective-permute-start | bytes 3145736 | tf_op jit(solution)/shard_map/ppermute | solution.py:234
  201.0 42.5 %collective-permute-start.14 = (bf16[1024,512]{1,0:T(8,128)(2,1)}, bf16[1024,512]{1,0:T(8,128)(2,1)}, u32[]{:S(2)}, u32[]{:S(2)}) collective-permute-start(bf16[1024,512]{1,0:T(8,128)(2,1)} %get-tuple-element.61), channel_id=1, source_target_pairs={{6,4},{4,2},{2,0},{7,5},{5,3},{3,1},{14,12},{12,10},{10,8},{15,13}... | collective-permute-start | bytes 3145736 | tf_op jit(solution)/shard_map/ppermute | solution.py:234
  216.2 33.1 %collective-permute-start.13 = (bf16[1024,512]{1,0:T(8,128)(2,1)S(1)}, bf16[1024,512]{1,0:T(8,128)(2,1)S(1)}, u32[]{:S(2)}, u32[]{:S(2)}) collective-permute-start(bf16[1024,512]{1,0:T(8,128)(2,1)S(1)} %copy-done.46), channel_id=1, source_target_pairs={{0,2},{2,4},{4,6},{1,3},{3,5},{5,7},{8,10},{10,12},{12,14},{9,11},... | collective-permute-start | bytes 3145736 | tf_op jit(solution)/shard_map/ppermute | solution.py:234
  221.1 77.7 %collective-permute-start.19 = (bf16[256,256]{1,0:T(8,128)(2,1)S(1)}, bf16[256,256]{1,0:T(8,128)(2,1)S(1)}, u32[]{:S(2)}, u32[]{:S(2)}) collective-permute-start(bf16[256,256]{1,0:T(8,128)(2,1)S(1)} %add_convert_fusion.32), channel_id=1, source_target_pairs={{0,2},{2,0},{4,6},{6,4},{1,3},{3,1},{5,7},{7,5},{8,10},{10,8},{12,... | collective-permute-start | bytes 393224 | tf_op jit(solution)/shard_map/ppermute | solution.py:205
  225.0 67.3 %collective-permute-start.23 = (bf16[1024,512]{1,0:T(8,128)(2,1)}, bf16[1024,512]{1,0:T(8,128)(2,1)}, u32[]{:S(2)}, u32[]{:S(2)}) collective-permute-start(bf16[1024,512]{1,0:T(8,128)(2,1)} %get-tuple-element.71), channel_id=1, source_target_pairs={{0,2},{2,4},{4,6},{1,3},{3,5},{5,7},{8,10},{10,12},{12,14},{9,11},... | collective-permute-start | bytes 3145736 | tf_op jit(solution)/shard_map/ppermute | solution.py:234
  243.5 48.8 %collective-permute-start.24 = (bf16[1024,512]{1,0:T(8,128)(2,1)}, bf16[1024,512]{1,0:T(8,128)(2,1)}, u32[]{:S(2)}, u32[]{:S(2)}) collective-permute-start(bf16[1024,512]{1,0:T(8,128)(2,1)} %get-tuple-element.72), channel_id=1, source_target_pairs={{6,4},{4,2},{2,0},{7,5},{5,3},{3,1},{14,12},{12,10},{10,8},{15,13}... | collective-permute-start | bytes 3145736 | tf_op jit(solution)/shard_map/ppermute | solution.py:234
  292.3 71.4 %collective-permute-start.25 = (bf16[1024,512]{1,0:T(8,128)(2,1)}, bf16[1024,512]{1,0:T(8,128)(2,1)}, u32[]{:S(2)}, u32[]{:S(2)}) collective-permute-start(bf16[1024,512]{1,0:T(8,128)(2,1)} %get-tuple-element.73), channel_id=1, source_target_pairs={{0,2},{2,4},{4,6},{1,3},{3,5},{5,7},{8,10},{10,12},{12,14},{9,11},... | collective-permute-start | bytes 3145736 | tf_op jit(solution)/shard_map/ppermute | solution.py:234
  297.5 66.2 %collective-permute-start.26 = (bf16[1024,512]{1,0:T(8,128)(2,1)}, bf16[1024,512]{1,0:T(8,128)(2,1)}, u32[]{:S(2)}, u32[]{:S(2)}) collective-permute-start(bf16[1024,512]{1,0:T(8,128)(2,1)} %get-tuple-element.74), channel_id=1, source_target_pairs={{6,4},{4,2},{2,0},{7,5},{5,3},{3,1},{14,12},{12,10},{10,8},{15,13}... | collective-permute-start | bytes 3145736 | tf_op jit(solution)/shard_map/ppermute | solution.py:234
  300.4 35.2 %collective-permute-start.22 = (bf16[512,256]{1,0:T(8,128)(2,1)S(1)}, bf16[512,256]{1,0:T(8,128)(2,1)}, u32[]{:S(2)}, u32[]{:S(2)}) collective-permute-start(bf16[512,256]{1,0:T(8,128)(2,1)S(1)} %pad_maximum_fusion.20), channel_id=1, source_target_pairs={{0,4},{2,6},{4,0},{6,2},{1,5},{3,7},{5,1},{7,3},{8,12},{10,14},{12... | collective-permute-start | bytes 786440 | tf_op jit(solution)/shard_map/ppermute | solution.py:205
  301.7 44.3 %collective-permute-start.20 = (bf16[1024,512]{1,0:T(8,128)(2,1)}, bf16[1024,512]{1,0:T(8,128)(2,1)}, u32[]{:S(2)}, u32[]{:S(2)}) collective-permute-start(bf16[1024,512]{1,0:T(8,128)(2,1)} %get-tuple-element.67), channel_id=1, source_target_pairs={{0,2},{2,4},{4,6},{1,3},{3,5},{5,7},{8,10},{10,12},{12,14},{9,11},... | collective-permute-start | bytes 3145736 | tf_op jit(solution)/shard_map/ppermute | solution.py:234
  307.1 44.0 %collective-permute-start.21 = (bf16[1024,512]{1,0:T(8,128)(2,1)}, bf16[1024,512]{1,0:T(8,128)(2,1)}, u32[]{:S(2)}, u32[]{:S(2)}) collective-permute-start(bf16[1024,512]{1,0:T(8,128)(2,1)} %get-tuple-element.68), channel_id=1, source_target_pairs={{6,4},{4,2},{2,0},{7,5},{5,3},{3,1},{14,12},{12,10},{10,8},{15,13}... | collective-permute-start | bytes 3145736 | tf_op jit(solution)/shard_map/ppermute | solution.py:234
  355.2 29.7 %collective-permute-start.28 = (bf16[1024,512]{1,0:T(8,128)(2,1)S(1)}, bf16[1024,512]{1,0:T(8,128)(2,1)S(1)}, u32[]{:S(2)}, u32[]{:S(2)}) collective-permute-start(bf16[1024,512]{1,0:T(8,128)(2,1)S(1)} %get-tuple-element.76), channel_id=1, source_target_pairs={{0,2},{2,4},{4,6},{1,3},{3,5},{5,7},{8,10},{10,12},{12,14},{9,11},... | collective-permute-start | bytes 3145736 | tf_op jit(solution)/shard_map/ppermute | solution.py:234
  362.4 25.7 %collective-permute-start.29 = (bf16[1024,512]{1,0:T(8,128)(2,1)S(1)}, bf16[1024,512]{1,0:T(8,128)(2,1)S(1)}, u32[]{:S(2)}, u32[]{:S(2)}) collective-permute-start(bf16[1024,512]{1,0:T(8,128)(2,1)S(1)} %get-tuple-element.77), channel_id=1, source_target_pairs={{6,4},{4,2},{2,0},{7,5},{5,3},{3,1},{14,12},{12,10},{10,8},{15,13}... | collective-permute-start | bytes 3145736 | tf_op jit(solution)/shard_map/ppermute | solution.py:234
  373.6 54.7 %collective-permute-start.31 = (bf16[1024,512]{1,0:T(8,128)(2,1)}, bf16[1024,512]{1,0:T(8,128)(2,1)}, u32[]{:S(2)}, u32[]{:S(2)}) collective-permute-start(bf16[1024,512]{1,0:T(8,128)(2,1)} %get-tuple-element.79), channel_id=1, source_target_pairs={{0,2},{2,4},{4,6},{1,3},{3,5},{5,7},{8,10},{10,12},{12,14},{9,11},... | collective-permute-start | bytes 3145736 | tf_op jit(solution)/shard_map/ppermute | solution.py:234
  379.2 49.1 %collective-permute-start.32 = (bf16[1024,512]{1,0:T(8,128)(2,1)}, bf16[1024,512]{1,0:T(8,128)(2,1)}, u32[]{:S(2)}, u32[]{:S(2)}) collective-permute-start(bf16[1024,512]{1,0:T(8,128)(2,1)} %get-tuple-element.80), channel_id=1, source_target_pairs={{6,4},{4,2},{2,0},{7,5},{5,3},{3,1},{14,12},{12,10},{10,8},{15,13}... | collective-permute-start | bytes 3145736 | tf_op jit(solution)/shard_map/ppermute | solution.py:234
  390.4 59.7 %collective-permute-start.35 = (bf16[1024,512]{1,0:T(8,128)(2,1)}, bf16[1024,512]{1,0:T(8,128)(2,1)}, u32[]{:S(2)}, u32[]{:S(2)}) collective-permute-start(bf16[1024,512]{1,0:T(8,128)(2,1)} %get-tuple-element.83), channel_id=1, source_target_pairs={{0,2},{2,4},{4,6},{1,3},{3,5},{5,7},{8,10},{10,12},{12,14},{9,11},... | collective-permute-start | bytes 3145736 | tf_op jit(solution)/shard_map/ppermute | solution.py:234
  394.5 57.4 %collective-permute-start.36 = (bf16[1024,512]{1,0:T(8,128)(2,1)}, bf16[1024,512]{1,0:T(8,128)(2,1)}, u32[]{:S(2)}, u32[]{:S(2)}) collective-permute-start(bf16[1024,512]{1,0:T(8,128)(2,1)} %get-tuple-element.84), channel_id=1, source_target_pairs={{6,4},{4,2},{2,0},{7,5},{5,3},{3,1},{14,12},{12,10},{10,8},{15,13}... | collective-permute-start | bytes 3145736 | tf_op jit(solution)/shard_map/ppermute | solution.py:234
  408.5 99.9 %collective-permute-start.39 = (bf16[256,2048]{1,0:T(8,128)(2,1)S(1)}, bf16[256,2048]{1,0:T(8,128)(2,1)S(1)}, u32[]{:S(2)}, u32[]{:S(2)}) collective-permute-start(bf16[256,2048]{1,0:T(8,128)(2,1)S(1)} %reduce-precision_convert_fusion.1), channel_id=1, source_target_pairs={{0,1},{1,0},{2,3},{3,2},{4,5},{5,4},{6,7},{7,6},{8,9},{9,8},{10,11... | collective-permute-start | bytes 3145736 | tf_op jit(solution)/shard_map/ppermute | solution.py:205
  430.8 45.3 %collective-permute-start.33 = (bf16[1024,512]{1,0:T(8,128)(2,1)S(1)}, bf16[1024,512]{1,0:T(8,128)(2,1)S(1)}, u32[]{:S(2)}, u32[]{:S(2)}) collective-permute-start(bf16[1024,512]{1,0:T(8,128)(2,1)S(1)} %get-tuple-element.81), channel_id=1, source_target_pairs={{0,2},{2,4},{4,6},{1,3},{3,5},{5,7},{8,10},{10,12},{12,14},{9,11},... | collective-permute-start | bytes 3145736 | tf_op jit(solution)/shard_map/ppermute | solution.py:234
  435.6 44.6 %collective-permute-start.34 = (bf16[1024,512]{1,0:T(8,128)(2,1)S(1)}, bf16[1024,512]{1,0:T(8,128)(2,1)}, u32[]{:S(2)}, u32[]{:S(2)}) collective-permute-start(bf16[1024,512]{1,0:T(8,128)(2,1)S(1)} %get-tuple-element.82), channel_id=1, source_target_pairs={{6,4},{4,2},{2,0},{7,5},{5,3},{3,1},{14,12},{12,10},{10,8},{15,13}... | collective-permute-start | bytes 3145736 | tf_op jit(solution)/shard_map/ppermute | solution.py:234
  472.6 35.8 %collective-permute-start.40 = (bf16[256,2048]{1,0:T(8,128)(2,1)S(1)}, bf16[256,2048]{1,0:T(8,128)(2,1)S(1)}, u32[]{:S(2)}, u32[]{:S(2)}) collective-permute-start(bf16[256,2048]{1,0:T(8,128)(2,1)S(1)} %reduce-precision_convert_fusion), channel_id=1, source_target_pairs={{0,1},{1,0},{2,3},{3,2},{4,5},{5,4},{6,7},{7,6},{8,9},{9,8},{10,11... | collective-permute-start | bytes 3145736 | tf_op jit(solution)/shard_map/ppermute | solution.py:205
  (70 other events, 1411.1 us)
